TPU v7x, 768 devices: a whole 4x8x12 slice. The times are simulated.
768 devices in a mesh: ctx: 48 (over y_lo, z), head: 16 (over y_hi, x, core).
Axes of the slice: x: 4, y: 8 (y_hi: 2, y_lo: 4; y = y_hi * 4 + y_lo), z: 12, core: 2. Of those that a mesh axis runs over, the one named last changes fastest.
Arguments:
- enc_states: bfloat16 [49152, 1024], P('ctx'), may hold values from -6 to 6
- local_gain: float32 [1024], replicated, may hold values from 0.1 to 1.9
- w_local: bfloat16 [1024, 16, 192], P(None, 'head'), may hold values from -10 to 10
- w_cross: bfloat16 [16, 64, 320], P('head'), may hold values from -50 to 50
- w_patch: bfloat16 [16, 64, 256], P('head'), may hold values from -0.75 to 0.75
- byte_patch: int32 [49152], P('ctx'), may hold values from 0 to 6143, as said below
- global_gain: float32 [4096], replicated, may hold values from 0.1 to 1.9
- w_global: bfloat16 [4096, 32, 384], P(None, 'head'), may hold values from -6 to 6
Outputs:
- context: bfloat16 [6144, 4096], P('ctx', 'head')
Inputs may be any that keep to these rules, and one draw needn't show every extreme that they name: byte_patch never falls and rises by at most one from byte to byte; every slab of 1024 bytes starts a new patch; the first patch of slab c has an index in [c * 128, (c + 1) * 128), so a slab holds 1 to 255 patches and both ends are reached; the first byte is in patch 0 and the last in patch 6144 - 1.
All inputs are finite; a program needn't handle non-finite values.
Results may differ from a plain program's by a relative error of at most 0.0095.
The roundings to bfloat16 on the way count: a program that leaves them out, or rounds other values in their place, can miss the bound.
Values may be sent and summed in bfloat16 or wider, within the bound.
No kernel may reach another device: no remote copies, remote signals or barrier semaphores. Data moves between devices by JAX's collectives and lax.ppermute only.
A program may use at most 64 MiB of HBM per device.

v0:
```python
import math

import jax
import jax.numpy as jnp
from jax import lax
from jax.sharding import PartitionSpec as P

DH_L = 64
DH = 128
W = 512
PATCH_LEN = 8
DG = 4096


neg_large = -1e30


def passed_along(block, axis, distance):
    devices = range(lax.axis_size(axis))
    route = [(i - distance, i) for i in devices if i - distance in devices]
    return lax.ppermute(block, axis, route)


def masked_softmax_apply(scores, allowed, values):
    row_peak = jnp.max(jnp.where(allowed, scores, neg_large), axis=-1, keepdims=True)
    weights = jnp.where(allowed, jnp.exp(scores - row_peak), 0.0)
    normalizer = jnp.sum(weights, axis=-1)
    normalizer = jnp.where(normalizer > 0, normalizer, 1.0)
    summed = jnp.einsum(
        "hqk,khd->qhd", weights.astype(jnp.bfloat16), values, preferred_element_type=jnp.float32
    )
    return summed / jnp.transpose(normalizer)[:, :, None]


def window_attend(queries, keys_vals, anchor):
    head_size = queries.shape[-1]
    scores = jnp.einsum(
        "qhd,khd->hqk", queries, keys_vals[:, :, :head_size], preferred_element_type=jnp.float32
    ) / math.sqrt(head_size)
    rows_at = lax.broadcasted_iota(jnp.int32, scores.shape, 1)
    cols_at = lax.broadcasted_iota(jnp.int32, scores.shape, 2)
    window = keys_vals.shape[0] - queries.shape[0]
    allowed = (cols_at > rows_at) & (cols_at <= rows_at + window) & (anchor + cols_at - window >= 0)
    return masked_softmax_apply(scores, allowed, keys_vals[:, :, head_size:])


def cross_attend(outputs, patch_ids, cross_weight, patch_weight, slot_count):
    head_size = outputs.shape[-1]
    first_id = patch_ids[0]
    local_ids = patch_ids - first_id
    member = local_ids[None, :] == jnp.arange(slot_count, dtype=jnp.int32)[:, None]
    counts = jnp.sum(member.astype(jnp.float32), axis=1)
    pooled = (
        jnp.einsum(
            "pb,bhd->phd", member.astype(jnp.bfloat16), outputs, preferred_element_type=jnp.float32
        )
        / jnp.maximum(counts, 1.0)[:, None, None]
    ).astype(jnp.bfloat16)
    cross_proj = jnp.einsum(
        "bhd,hde->bhe", outputs, cross_weight, preferred_element_type=jnp.float32
    ).astype(jnp.bfloat16)
    scores = jnp.einsum(
        "phd,bhd->hpb", pooled, cross_proj[:, :, :head_size], preferred_element_type=jnp.float32
    ) / math.sqrt(head_size)
    allowed = member[None]
    attended = masked_softmax_apply(scores, allowed, cross_proj[:, :, head_size:])
    lifted = jnp.einsum("phd,hde->phe", pooled, patch_weight, preferred_element_type=jnp.float32)
    patch_rows = (lifted + attended).astype(jnp.bfloat16)
    return (patch_rows.reshape(slot_count, -1), first_id, patch_ids[-1] - first_id + 1)


def local(enc_states, local_gain, w_local, w_cross, w_patch, byte_patch, global_gain, w_global):
    byte_count = enc_states.shape[0]
    quota = byte_count // PATCH_LEN
    ctx_pos = lax.axis_index("ctx")
    states = enc_states.astype(jnp.float32)
    normed = (
        states * lax.rsqrt(jnp.mean(states * states, axis=-1, keepdims=True) + 1e-05) * local_gain
    ).astype(jnp.bfloat16)
    local_proj = jnp.einsum(
        "bd,dhe->bhe", normed, w_local, preferred_element_type=jnp.float32
    ).astype(jnp.bfloat16)
    rim_rows = passed_along(local_proj[byte_count - W :, :, DH_L:], "ctx", 1)
    keys_all = jnp.concatenate([rim_rows, local_proj[:, :, DH_L:]], axis=0)
    block_rows = min(512, byte_count)
    outputs_list = []
    for first_row in range(0, byte_count, block_rows):
        attended = window_attend(
            local_proj[first_row : first_row + block_rows, :, :DH_L],
            keys_all[first_row : first_row + block_rows + W],
            ctx_pos * byte_count + first_row,
        )
        outputs_list.append(attended.astype(jnp.bfloat16))
    local_out = jnp.concatenate(outputs_list, axis=0)
    slot_count = 2 * quota
    local_rows, first_id, patch_count = cross_attend(
        local_out, byte_patch, w_cross, w_patch, slot_count
    )
    slot_index = jnp.arange(slot_count, dtype=jnp.int32)[:, None]
    local_rows = jnp.where(slot_index < patch_count, local_rows, jnp.zeros_like(local_rows))
    excess = first_id - ctx_pos * quota
    padded = jnp.concatenate(
        [jnp.zeros((quota, local_rows.shape[1]), jnp.bfloat16), local_rows], axis=0
    )
    kept_rows = lax.dynamic_slice_in_dim(padded, quota - excess, quota, 0)
    leaving = lax.dynamic_slice_in_dim(local_rows, quota - excess, quota, 0)
    arriving = passed_along(leaving, "ctx", 1)
    slab_rows = kept_rows + arriving
    head_total = w_global.shape[1]
    flat_weight = w_global.reshape(DG, head_total * 3 * DH)
    piece_f = lax.all_gather(slab_rows, "head", axis=1, tiled=True).astype(jnp.float32)
    scaled = (piece_f * global_gain).astype(jnp.bfloat16)
    summed = jnp.dot(scaled, flat_weight, preferred_element_type=jnp.float32)
    squares = jnp.sum(piece_f * piece_f, axis=1)
    row_scale = lax.rsqrt(squares / DG + 1e-05)
    global_proj = (
        (summed * row_scale[:, None]).astype(jnp.bfloat16).reshape(quota, head_total, 3 * DH)
    )
    queries = global_proj[:, :, :DH]
    keys_vals = global_proj[:, :, DH:]
    query_base = ctx_pos * quota
    shard_piece = lax.all_gather(keys_vals, "ctx", axis=0, tiled=True)
    row_peak = jnp.full((head_total, quota), neg_large, jnp.float32)
    scores = jnp.einsum(
        "qhd,khd->hqk", queries, shard_piece[:, :, :DH], preferred_element_type=jnp.float32
    ) / math.sqrt(DH)
    rows_at = query_base + lax.broadcasted_iota(jnp.int32, scores.shape, 1)
    cols_at = lax.broadcasted_iota(jnp.int32, scores.shape, 2)
    allowed = cols_at <= rows_at
    new_peak = jnp.maximum(row_peak, jnp.max(jnp.where(allowed, scores, neg_large), axis=-1))
    weights = jnp.where(allowed, jnp.exp(scores - new_peak[:, :, None]), 0.0)
    normalizer = jnp.sum(weights, axis=-1)
    added = jnp.einsum(
        "hqk,khd->qhd",
        weights.astype(jnp.bfloat16),
        shard_piece[:, :, DH:],
        preferred_element_type=jnp.float32,
    )
    summed_vals = added
    row_peak, normalizer, summed_vals = (new_peak, normalizer, summed_vals)
    context = (summed_vals / jnp.transpose(normalizer)[:, :, None]).astype(jnp.bfloat16)
    return context.reshape(quota, head_total * DH)


def solution(mesh):
    in_specs = (
        P("ctx", None),
        P(),
        P(None, "head", None),
        P("head", None, None),
        P("head", None, None),
        P("ctx"),
        P(),
        P(None, "head", None),
    )
    out_specs = P("ctx", "head")
    return jax.shard_map(local, mesh=mesh, in_specs=in_specs, out_specs=out_specs, check_vma=False)
```

profile of v0, /device:TPU:2, one launch (start us, length us, event | category | flops | bytes accessed | tf_op | source)
XLA Modules:
  0.0 360.9 jit_solution(4124719699332222841)
XLA Ops:
  6.5 0.0 copy-start
  6.5 0.0 copy-start.1
  6.5 0.0 copy-start.7
  6.5 0.0 all-gather.3.cloned.1.call-start
  6.5 2.2 fusion.2
  8.8 0.0 copy-done
  8.8 0.1 copy-done.1
  8.9 0.0 copy-done.7
  8.9 0.9 fusion.29
  9.8 0.0 copy-start.5
  9.9 4.3 %collective-permute-start = (bf16[512,1,128]{0,2,1:T(8,128)(2,1)S(1)}, bf16[512,1,128]{0,2,1:T(8,128)(2,1)S(1)}, u32[]{:S(2)}, u32[]{:S(2)}) collective-permute-start(bf16[512,1,128]{0,2,1:T(8,128)(2,1)S(1)} %slice.69), channel_id=1, source_target_pairs={{0,16},{16,32},{32,48},{48,64},{64,80},{80,96},{96,112},{112,128},... | collective-permute-start | bytes 393224 | tf_op jit(solution)/shard_map/ppermute | solution.py:21
  14.2 0.5 fusion.76
  14.6 0.0 copy-done.5
  14.6 0.6 fusion.97
  15.2 0.7 broadcast_subtract_fusion
  17.3 0.2 convert_reduce_fusion
  18.2 0.0 collective-permute-done
  18.2 1.1 select_reduce_fusion.2
  19.4 2.0 fusion.21
  21.3 0.8 fusion.46
  22.2 0.0 copy-start.2
  22.2 0.8 fusion.43
  23.0 0.3 fusion.47
  23.4 0.0 copy-done.2
  23.4 0.4 fusion.25
  23.8 0.4 select_reduce_fusion.3
  24.2 0.0 copy-start.3
  24.2 0.4 fusion.68
  24.6 0.4 fusion.48
  25.0 0.0 copy-done.3
  25.0 0.2 fusion.49
  25.2 4.3 %collective-permute-start.1 = (bf16[128,256]{1,0:T(8,128)(2,1)S(1)}, bf16[128,256]{1,0:T(8,128)(2,1)S(1)}, u32[]{:S(2)}, u32[]{:S(2)}) collective-permute-start(bf16[128,256]{1,0:T(8,128)(2,1)S(1)} %constant_dynamic-slice_fusion), channel_id=1, source_target_pairs={{0,16},{16,32},{32,48},{48,64},{64,80},{80,96},{96,112},{112,128},... | collective-permute-start | bytes 196616 | tf_op jit(solution)/shard_map/ppermute | solution.py:21
  29.5 1.9 collective-permute-done.1
  31.4 0.7 fusion.83
  32.1 0.0 all-gather.3.cloned.1.call-update
  32.1 0.2 all-gather.5.cloned.1.call-start
  32.4 0.0 copy-start.4
  32.4 6.5 %copy.18 = bf16[512,8,2,384]{3,1,2,0:T(8,128)(2,1)} copy(bf16[512,8,2,384]{3,2,1,0:T(2,128)(2,1)} %bitcast.109) | data formatting | bytes 12582912
  38.9 63.9 %all-gather.3.cloned.1.call-done = bf16[128,4096]{1,0:T(8,128)(2,1)} async-done(((bf16[128,256]{1,0:T(8,128)(2,1)}), bf16[128,4096]{1,0:T(8,128)(2,1)}) %all-gather.3.cloned.1.call-update) | async-done | bytes 1048592 | tf_op jit(solution)/shard_map/all_gather | solution.py:111
  102.9 1.5 fusion.13
  104.4 0.0 copy-done.4
  104.4 4.1 %fusion.32 = bf16[128,768]{1,0:T(8,128)(2,1)S(1)} fusion(bf16[4096,768]{1,0:T(8,128)(2,1)} %bitcast.108, bf16[128,4096]{1,0:T(8,128)(2,1)} %all-gather.3.cloned.1.call-done, f32[4096]{0:T(1024)S(1)} %copy-done.4, f32[128]{0:T(128)S(1)} %add_rsqrt_fusion.1), kind=kOutput, calls=%fused_computation.43 | convolution fusion | flops 807075840 | bytes 7553536 | tf_op jit(solution)/shard_map/dot_general | solution.py:113
  108.5 0.1 reshape.193
  108.6 0.1 slice.77
  108.7 0.7 copy.16
  109.3 0.0 all-gather.5.cloned.1.call-update
  109.4 235.4 %all-gather.5.cloned.1.call-done = bf16[6144,2,256]{2,0,1:T(8,128)(2,1)} async-done(((bf16[128,2,256]{2,0,1:T(8,128)(2,1)}), bf16[6144,2,256]{2,0,1:T(8,128)(2,1)}) %all-gather.5.cloned.1.call-update) | async-done | bytes 6291472 | tf_op jit(solution)/shard_map/all_gather | solution.py:122
  344.8 3.6 select_reduce_fusion
  348.4 0.0 copy-start.6
  348.4 1.6 fusion
  350.0 1.2 copy-done.6
  351.2 2.1 fusion.55
  353.3 0.7 copy.13
  (15 shorter events, 0.2 us)
Async XLA Ops:
  6.5 2.2 copy-start
  6.5 2.4 copy-start.1
  6.5 2.4 copy-start.7
  6.5 96.3 %all-gather.3.cloned.1.call-start = ((), (), s32[]{:S(2)}) async-start(), calls=%async_computation | async-start | bytes 1114112 | tf_op jit(solution)/shard_map/all_gather | solution.py:111
  9.8 4.8 %copy-start.5 = (s32[1024]{0:T(1024)S(1)}, s32[1024]{0:T(1024)}, u32[]{:S(2)}) copy-start(s32[1024]{0:T(1024)} %param.13) | copy-start | bytes 12292
  9.9 8.4 %collective-permute-start = (bf16[512,1,128]{0,2,1:T(8,128)(2,1)S(1)}, bf16[512,1,128]{0,2,1:T(8,128)(2,1)S(1)}, u32[]{:S(2)}, u32[]{:S(2)}) collective-permute-start(bf16[512,1,128]{0,2,1:T(8,128)(2,1)S(1)} %slice.69), channel_id=1, source_target_pairs={{0,16},{16,32},{32,48},{48,64},{64,80},{80,96},{96,112},{112,128},... | collective-permute-start | bytes 393224 | tf_op jit(solution)/shard_map/ppermute | solution.py:21
  22.2 1.2 copy-start.2
  24.2 0.8 copy-start.3
  25.2 6.2 %collective-permute-start.1 = (bf16[128,256]{1,0:T(8,128)(2,1)S(1)}, bf16[128,256]{1,0:T(8,128)(2,1)S(1)}, u32[]{:S(2)}, u32[]{:S(2)}) collective-permute-start(bf16[128,256]{1,0:T(8,128)(2,1)S(1)} %constant_dynamic-slice_fusion), channel_id=1, source_target_pairs={{0,16},{16,32},{32,48},{48,64},{64,80},{80,96},{96,112},{112,128},... | collective-permute-start | bytes 196616 | tf_op jit(solution)/shard_map/ppermute | solution.py:21
  32.1 312.7 %all-gather.5.cloned.1.call-start = ((), (), s32[]{:S(2)}) async-start(), calls=%async_computation.1 | async-start | bytes 6422528 | tf_op jit(solution)/shard_map/all_gather | solution.py:122
  32.4 72.0 %copy-start.4 = (f32[4096]{0:T(1024)S(1)}, f32[4096]{0:T(1024)}, u32[]{:S(2)}) copy-start(f32[4096]{0:T(1024)} %param.14) | copy-start | bytes 49156
  348.4 2.8 copy-start.6
Sparse Core Ops, SparseCore 0:
  32.3 70.5 all-gather.2
  109.5 235.3 all-gather.4
where the time goes:
time: 361 us
  waiting for transfers between devices  301 us (83%)
  matrix products  15.7 us (4%)
  between operations  15.7 us (4%)
  local copies, waits for them, and re-layouts  10.1 us (3%)
  other arithmetic  9.36 us (3%)
  starting transfers between devices  8.77 us (2%)
    all_gather x1, waiting for transfers between devices, local(): shard_piece = lax.all_gather(keys_vals, 'ctx', axis=0, tiled=True)  235 us
    all_gather x1, waiting for transfers between devices, local(): lax.all_gather(slab_rows, 'head', axis=1, tiled=True).astype(jnp.float32)  63.9 us
    ppermute x2, starting transfers between devices, passed_along(): return lax.ppermute(block, axis, route)  8.55 us
    unnamed x18, local copies, waits for them, and re-layouts  8.49 us
  transfers between devices with their start and end apart: 4, of which 3 were waited for; matrix products, arithmetic and copies ran while one was open for 2% of the time, Pallas kernels for 0%

commit v1 on v0

--- a/solution.py
+++ b/solution.py
@@ -1,9 +1,17 @@
+import functools
 import math
 
 import jax
 import jax.numpy as jnp
 from jax import lax
-from jax.sharding import PartitionSpec as P
+from jax.experimental import pallas as pl
+from jax.experimental.pallas import tpu as pltpu
+from jax.sharding import Mesh, PartitionSpec as P
+
+CTX = ("yl", "zh", "zl")
+HEAD = ("yh", "x", "core")
+Y_LO, Z_HALF, Z_PAIR, Y_HI, X, CORE = 4, 6, 2, 2, 4, 2
+N_CTX = Y_LO * Z_HALF * Z_PAIR
 
 DH_L = 64
 DH = 128
@@ -16,7 +24,7 @@
 
 
 def passed_along(block, axis, distance):
-    devices = range(lax.axis_size(axis))
+    devices = range(N_CTX)
     route = [(i - distance, i) for i in devices if i - distance in devices]
     return lax.ppermute(block, axis, route)
 
@@ -69,10 +77,124 @@
     return (patch_rows.reshape(slot_count, -1), first_id, patch_ids[-1] - first_id + 1)
 
 
+def project_kernel(pos_ref, own_ref, other_ref, gain_ref, w_ref, out_ref):
+    core = pos_ref[2]
+    rows = own_ref.shape[2]
+    width = own_ref.shape[3]
+    total = jnp.zeros((rows, w_ref.shape[1]), jnp.float32)
+    squares = jnp.zeros((rows, 1), jnp.float32)
+    for block_ref, block_core in ((own_ref, core), (other_ref, 1 - core)):
+        for x in range(X):
+            for yh in range(Y_HI):
+                block = block_ref[x, yh].astype(jnp.float32)
+                first = pl.multiple_of((yh * X * CORE + x * CORE + block_core) * width, width)
+                gain = gain_ref[:, pl.ds(first, width)]
+                squares = squares + jnp.sum(block * block, axis=1, keepdims=True)
+                total = total + jnp.dot(
+                    (block * gain).astype(jnp.bfloat16),
+                    w_ref[pl.ds(first, width), :],
+                    preferred_element_type=jnp.float32,
+                )
+    out_ref[...] = (total * lax.rsqrt(squares / DG + 1e-05)).astype(jnp.bfloat16)
+
+
+def attend_kernel(pos_ref, q_ref, kv_ref, out_ref, vt_ref, s_ref):
+    y = pos_ref[0]
+    zh = pos_ref[1]
+    key_count = kv_ref.shape[0]
+    rows = 2 * q_ref.shape[1]
+    half = q_ref.shape[1]
+    scale = math.log2(math.e) / math.sqrt(DH)
+    vt_ref[...] = kv_ref[:, DH:].T
+    chunk = 512
+
+    def attend(yy, masked):
+        queries = q_ref[pl.ds(2 * yy, 2)].reshape(rows, DH)
+        peak = jnp.full((1, rows), neg_large, jnp.float32)
+        for first in range(0, key_count, chunk):
+            scores = lax.dot_general(
+                kv_ref[first : first + chunk, :DH],
+                queries,
+                (((1,), (1,)), ((), ())),
+                preferred_element_type=jnp.float32,
+            ) * scale
+            if masked:
+                key_at = first + lax.broadcasted_iota(jnp.int32, scores.shape, 0)
+                query_at = zh * rows + lax.broadcasted_iota(jnp.int32, scores.shape, 1)
+                scores = jnp.where(key_at <= query_at, scores, neg_large)
+            s_ref[first : first + chunk] = scores
+            peak = jnp.maximum(peak, jnp.max(scores, axis=0, keepdims=True))
+        normalizer = jnp.zeros((1, rows), jnp.float32)
+        summed = jnp.zeros((DH, rows), jnp.float32)
+        for first in range(0, key_count, chunk):
+            weights = jnp.exp2(s_ref[first : first + chunk] - peak)
+            normalizer = normalizer + jnp.sum(weights, axis=0, keepdims=True)
+            summed = summed + jnp.dot(
+                vt_ref[:, first : first + chunk],
+                weights.astype(jnp.bfloat16),
+                preferred_element_type=jnp.float32,
+            )
+        summed = (summed / normalizer).astype(jnp.bfloat16)
+        level = peak + jnp.log2(normalizer)
+        high = level.astype(jnp.bfloat16)
+        rest = level - high.astype(jnp.float32)
+        mid = rest.astype(jnp.bfloat16)
+        low = (rest - mid.astype(jnp.float32)).astype(jnp.bfloat16)
+        stats = jnp.concatenate(
+            [high, mid, low, jnp.zeros((13, rows), jnp.bfloat16)], axis=0
+        )
+        for part in range(2):
+            lanes = slice(part * half, (part + 1) * half)
+            out_ref[2 * yy + part, :DH, :] = summed[:, lanes]
+            out_ref[2 * yy + part, DH:, :] = stats[:, lanes]
+
+    for yy in range(Y_LO):
+
+        @pl.when(yy < y)
+        def _():
+            row_at = lax.broadcasted_iota(jnp.int32, (16, half), 0)
+            stats = jnp.where(row_at == 0, neg_large, 0.0).astype(jnp.bfloat16)
+            for part in range(2):
+                out_ref[2 * yy + part, :DH, :] = jnp.zeros((DH, half), jnp.bfloat16)
+                out_ref[2 * yy + part, DH:, :] = stats
+
+        @pl.when(yy == y)
+        def _():
+            attend(yy, True)
+
+        @pl.when(yy > y)
+        def _():
+            attend(yy, False)
+
+
+def merge_kernel(parts_ref, out_ref):
+    for head in range(2):
+        levels = []
+        for yy in range(Y_LO):
+            stats = parts_ref[2 * yy + head, DH:, :].astype(jnp.float32)
+            levels.append(stats[0:1] + stats[1:2] + stats[2:3])
+        peak = functools.reduce(jnp.maximum, levels)
+        total = jnp.zeros((DH, out_ref.shape[0]), jnp.float32)
+        normalizer = jnp.zeros((1, out_ref.shape[0]), jnp.float32)
+        for yy in range(Y_LO):
+            share = jnp.exp2(levels[yy] - peak)
+            normalizer = normalizer + share
+            total = total + share * parts_ref[2 * yy + head, :DH, :].astype(jnp.float32)
+        out_ref[:, head * DH : (head + 1) * DH] = (total / normalizer).T.astype(jnp.bfloat16)
+
+
+VMEM = pl.BlockSpec(memory_space=pltpu.VMEM)
+SMEM = pl.BlockSpec(memory_space=pltpu.SMEM)
+
+
+def all_to_all_of(block, axes):
+    return lax.all_to_all(block, axes, 0, 0, tiled=True)
+
+
 def local(enc_states, local_gain, w_local, w_cross, w_patch, byte_patch, global_gain, w_global):
     byte_count = enc_states.shape[0]
     quota = byte_count // PATCH_LEN
-    ctx_pos = lax.axis_index("ctx")
+    ctx_pos = lax.axis_index(CTX)
     states = enc_states.astype(jnp.float32)
     normed = (
         states * lax.rsqrt(jnp.mean(states * states, axis=-1, keepdims=True) + 1e-05) * local_gain
@@ -80,7 +202,7 @@
     local_proj = jnp.einsum(
         "bd,dhe->bhe", normed, w_local, preferred_element_type=jnp.float32
     ).astype(jnp.bfloat16)
-    rim_rows = passed_along(local_proj[byte_count - W :, :, DH_L:], "ctx", 1)
+    rim_rows = passed_along(local_proj[byte_count - W :, :, DH_L:], CTX, 1)
     keys_all = jnp.concatenate([rim_rows, local_proj[:, :, DH_L:]], axis=0)
     block_rows = min(512, byte_count)
     outputs_list = []
@@ -104,54 +226,75 @@
     )
     kept_rows = lax.dynamic_slice_in_dim(padded, quota - excess, quota, 0)
     leaving = lax.dynamic_slice_in_dim(local_rows, quota - excess, quota, 0)
-    arriving = passed_along(leaving, "ctx", 1)
+    arriving = passed_along(leaving, CTX, 1)
     slab_rows = kept_rows + arriving
     head_total = w_global.shape[1]
     flat_weight = w_global.reshape(DG, head_total * 3 * DH)
-    piece_f = lax.all_gather(slab_rows, "head", axis=1, tiled=True).astype(jnp.float32)
-    scaled = (piece_f * global_gain).astype(jnp.bfloat16)
-    summed = jnp.dot(scaled, flat_weight, preferred_element_type=jnp.float32)
-    squares = jnp.sum(piece_f * piece_f, axis=1)
-    row_scale = lax.rsqrt(squares / DG + 1e-05)
-    global_proj = (
-        (summed * row_scale[:, None]).astype(jnp.bfloat16).reshape(quota, head_total, 3 * DH)
-    )
-    queries = global_proj[:, :, :DH]
-    keys_vals = global_proj[:, :, DH:]
-    query_base = ctx_pos * quota
-    shard_piece = lax.all_gather(keys_vals, "ctx", axis=0, tiled=True)
-    row_peak = jnp.full((head_total, quota), neg_large, jnp.float32)
-    scores = jnp.einsum(
-        "qhd,khd->hqk", queries, shard_piece[:, :, :DH], preferred_element_type=jnp.float32
-    ) / math.sqrt(DH)
-    rows_at = query_base + lax.broadcasted_iota(jnp.int32, scores.shape, 1)
-    cols_at = lax.broadcasted_iota(jnp.int32, scores.shape, 2)
-    allowed = cols_at <= rows_at
-    new_peak = jnp.maximum(row_peak, jnp.max(jnp.where(allowed, scores, neg_large), axis=-1))
-    weights = jnp.where(allowed, jnp.exp(scores - new_peak[:, :, None]), 0.0)
-    normalizer = jnp.sum(weights, axis=-1)
-    added = jnp.einsum(
-        "hqk,khd->qhd",
-        weights.astype(jnp.bfloat16),
-        shard_piece[:, :, DH:],
-        preferred_element_type=jnp.float32,
-    )
-    summed_vals = added
-    row_peak, normalizer, summed_vals = (new_peak, normalizer, summed_vals)
-    context = (summed_vals / jnp.transpose(normalizer)[:, :, None]).astype(jnp.bfloat16)
-    return context.reshape(quota, head_total * DH)
+    y = lax.axis_index("yl")
+    zh = lax.axis_index("zh")
+    zl = lax.axis_index("zl")
+    pos = jnp.stack([y, zh, lax.axis_index("core")]).astype(jnp.int32)
+    pair_rows = lax.all_gather(slab_rows, "yh", axis=0)
+    own_rows = all_to_all_of(jnp.broadcast_to(pair_rows[None], (X,) + pair_rows.shape), "x")
+    other_rows = lax.ppermute(own_rows, "core", [(0, 1), (1, 0)])
+    global_proj = pl.pallas_call(
+        project_kernel,
+        out_shape=jax.ShapeDtypeStruct((quota, head_total * 3 * DH), jnp.bfloat16),
+        in_specs=[SMEM, VMEM, VMEM, VMEM, VMEM],
+        out_specs=VMEM,
+        compiler_params=pltpu.CompilerParams(vmem_limit_bytes=32 << 20),
+        cost_estimate=pl.CostEstimate(
+            flops=2 * quota * DG * head_total * 3 * DH, bytes_accessed=8 << 20, transcendentals=0
+        ),
+        name="project",
+    )(pos, own_rows, other_rows, global_gain.reshape(1, DG), flat_weight)
+    first_kv = global_proj[:, DH : 3 * DH]
+    second_kv = global_proj[:, 4 * DH : 6 * DH]
+    swapped = lax.ppermute(jnp.where(zl == 0, second_kv, first_kv), "zl", [(0, 1), (1, 0)])
+    queries = jnp.stack([global_proj[:, :DH], global_proj[:, 3 * DH : 4 * DH]])
+    queries = jnp.broadcast_to(queries[None], (Y_LO,) + queries.shape)
+    queries = queries.reshape(Y_LO * Z_PAIR, quota, DH)
+    queries = all_to_all_of(queries, ("yl", "zl"))
+    pair_kv = jnp.concatenate(
+        [jnp.where(zl == 0, first_kv, swapped), jnp.where(zl == 0, swapped, second_kv)], axis=0
+    )
+    keys_vals = lax.all_gather(pair_kv, "zh", axis=0, tiled=True)
+    key_count = keys_vals.shape[0]
+    partial_out = pl.pallas_call(
+        attend_kernel,
+        out_shape=jax.ShapeDtypeStruct((Y_LO * Z_PAIR, DH + 16, quota), jnp.bfloat16),
+        in_specs=[SMEM, VMEM, VMEM],
+        out_specs=VMEM,
+        scratch_shapes=[
+            pltpu.VMEM((DH, key_count), jnp.bfloat16),
+            pltpu.VMEM((key_count, 2 * quota), jnp.float32),
+        ],
+        compiler_params=pltpu.CompilerParams(vmem_limit_bytes=32 << 20),
+        name="attend",
+    )(pos, queries, keys_vals)
+    parts = all_to_all_of(partial_out, ("yl", "zl"))
+    return pl.pallas_call(
+        merge_kernel,
+        out_shape=jax.ShapeDtypeStruct((quota, head_total * DH), jnp.bfloat16),
+        in_specs=[VMEM],
+        out_specs=VMEM,
+        name="merge",
+    )(parts)
 
 
 def solution(mesh):
+    split = Mesh(
+        mesh.devices.reshape(Y_LO, Z_HALF, Z_PAIR, Y_HI, X, CORE), CTX + HEAD
+    )
     in_specs = (
-        P("ctx", None),
+        P(CTX, None),
         P(),
-        P(None, "head", None),
-        P("head", None, None),
-        P("head", None, None),
-        P("ctx"),
+        P(None, HEAD, None),
+        P(HEAD, None, None),
+        P(HEAD, None, None),
+        P(CTX),
         P(),
-        P(None, "head", None),
-    )
-    out_specs = P("ctx", "head")
-    return jax.shard_map(local, mesh=mesh, in_specs=in_specs, out_specs=out_specs, check_vma=False)
+        P(None, HEAD, None),
+    )
+    out_specs = P(CTX, HEAD)
+    return jax.shard_map(local, mesh=split, in_specs=in_specs, out_specs=out_specs, check_vma=False)

time: 361 us -> 119 us (0.33)
  waiting for transfers between devices: 301 us -> 1.89 us
  blocking collectives: 0 us -> 61.1 us
  starting transfers between devices: 8.77 us -> 27.7 us
  between operations: 15.7 us -> 2.27 us
  matrix products: 15.7 us -> 5.81 us
  Pallas kernels: 0 us -> 8.26 us
  local copies, waits for them, and re-layouts: 10.1 us -> 5.43 us
  other arithmetic: 9.36 us -> 5.61 us
    all_gather x2 -> x0, waiting for transfers between devices: 299 us -> none  [the longest x1 235 us: local(): shard_piece = lax.all_gather(keys_vals, 'ctx', axis=0, tiled=True)]
    all_gather x0 -> x2, blocking collectives: none -> 33 us  [the longest x1 24.1 us: local(): keys_vals = lax.all_gather(pair_kv, 'zh', axis=0, tiled=True)]
    all_to_all x0 -> x2, blocking collectives: none -> 28.1 us  [all_to_all_of(): return lax.all_to_all(block, axes, 0, 0, tiled=True)]
    all_to_all x0 -> x1, starting transfers between devices: none -> 13.3 us  [all_to_all_of(): return lax.all_to_all(block, axes, 0, 0, tiled=True)]
    dot_general x3 -> x0, matrix products: 9.81 us -> none  [the longest x1 4.11 us: local(): summed = jnp.dot(scaled, flat_weight, preferred_element_type=jnp.float32)]
    pallas_call x0 -> x3, Pallas kernels: none -> 8.26 us  [the longest x1 4.82 us: local(): pl.pallas_call(attend_kernel, out_shape=jax.ShapeDtypeStruct((Y_LO * Z_PA...]
    ppermute x0 -> x2, starting transfers between devices: none -> 5.87 us  [the longest x1 3.96 us: local(): lax.ppermute(jnp.where(zl == 0, second_kv, first_kv), 'zl', [(0, 1), (1,...]
    unnamed x18 -> x15, local copies, waits for them, and re-layouts: 8.49 us -> 4.02 us
  transfers between devices with their start and end apart: 4 -> 5, of which waited for: 3 -> 1; matrix products, arithmetic and copies ran while one was open for 2% -> 6% of each run, Pallas kernels for 0% -> 0%
where the time goes in v1:
time: 119 us; the launch traced here: 118 us
  blocking collectives  61.1 us (51%)
  starting transfers between devices  27.7 us (23%)
  Pallas kernels  8.26 us (7%)
  matrix products  5.81 us (5%)
  other arithmetic  5.61 us (5%)
  local copies, waits for them, and re-layouts  5.43 us (5%)
  between operations  2.27 us (2%)
  waiting for transfers between devices  1.89 us (2%)
    all_to_all x2, blocking collectives, all_to_all_of(): return lax.all_to_all(block, axes, 0, 0, tiled=True)  28.1 us
    all_gather x1, blocking collectives, local(): keys_vals = lax.all_gather(pair_kv, 'zh', axis=0, tiled=True)  24.1 us
    all_to_all x1, starting transfers between devices, all_to_all_of(): return lax.all_to_all(block, axes, 0, 0, tiled=True)  13.3 us
    all_gather x1, blocking collectives, local(): pair_rows = lax.all_gather(slab_rows, 'yh', axis=0)  8.85 us
    ppermute x2, starting transfers between devices, passed_along(): return lax.ppermute(block, axis, route)  8.57 us
    pallas_call x1, Pallas kernels, local(): pl.pallas_call(attend_kernel, out_shape=jax.ShapeDtypeStruct((Y_LO * Z_PA...  4.82 us
    unnamed x15, local copies, waits for them, and re-layouts  4.02 us
    ppermute x1, starting transfers between devices, local(): lax.ppermute(jnp.where(zl == 0, second_kv, first_kv), 'zl', [(0, 1), (1,...  3.96 us
  transfers between devices with their start and end apart: 5, of which 1 were waited for; matrix products, arithmetic and copies ran while one was open for 6% of the time, Pallas kernels for 0%

profile of v1, /device:TPU:2, one launch (start us, length us, event | category | flops | bytes accessed | tf_op | source)
XLA Modules:
  0.0 118.1 jit_solution(8699491174926291552)
XLA Ops:
  0.0 0.0 copy-start
  0.0 0.0 copy-start.2
  0.0 0.0 copy-start.6
  0.0 2.2 %fusion = f32[1024]{0:T(1024)S(1)} fusion(bf16[1024,1024]{1,0:T(8,128)(2,1)} %param.8), kind=kLoop, calls=%fused_computation.2 | loop fusion | flops 3144704 | bytes 2101248 | tf_op jit(solution)/shard_map/reduce_sum | solution.py:200
  2.2 0.0 copy-done
  2.3 0.1 copy-done.2
  2.4 0.0 copy-done.6
  2.4 0.9 fusion.18
  3.3 0.0 copy-start.5
  3.3 4.3 %collective-permute-start = (bf16[512,1,128]{0,2,1:T(8,128)(2,1)S(1)}, bf16[512,1,128]{0,2,1:T(8,128)(2,1)S(1)}, u32[]{:S(2)}, u32[]{:S(2)}) collective-permute-start(bf16[512,1,128]{0,2,1:T(8,128)(2,1)S(1)} %slice.69), channel_id=1, source_target_pairs={{0,16},{16,32},{32,48},{48,64},{64,80},{80,96},{96,112},{112,128},... | collective-permute-start | bytes 393224 | tf_op jit(solution)/shard_map/ppermute | solution.py:29
  7.6 0.5 fusion.47
  8.1 0.0 copy-done.5
  8.1 0.6 fusion.66
  8.7 0.6 broadcast_subtract_fusion
  10.6 0.2 convert_reduce_fusion
  11.5 0.0 collective-permute-done
  11.5 1.1 select_reduce_fusion.1
  12.6 1.9 %fusion.10 = (f32[512]{0:T(512)S(1)}, f32[512]{0:T(512)S(1)}) fusion(f32[512,1024]{1,0:T(8,128)S(1)} %get-tuple-element.15, f32[512]{0:T(512)S(1)} %get-tuple-element.7, pred[1024]{0:T(1024)(128)(4,1)S(1)} %get-tuple-element.19, s32[512]{0:T(512)S(1)} %iota_add_fusion, f32[512]{0:T(512)S(1)} %get-tuple-element.8, f32[512,1024]{1,0:T(8,128)S(1)} %fusion.47, ...), kind=kLoop, calls=%fused_computation.19 | loop fusion | flops 6814720 | bytes 4206592 | tf_op jit(solution)/shard_map/reduce_sum | solution.py:35
  14.6 0.8 fusion.29
  15.4 0.0 copy-start.3
  15.4 0.8 fusion.26
  16.3 0.3 fusion.30
  16.6 0.0 copy-done.3
  16.6 0.4 fusion.14
  16.9 0.4 select_reduce_fusion.2
  17.4 0.0 copy-start.4
  17.4 0.4 fusion.39
  17.8 0.4 fusion.31
  18.2 0.0 copy-done.4
  18.2 0.2 fusion.32
  18.4 4.3 %collective-permute-start.1 = (bf16[128,256]{1,0:T(8,128)(2,1)S(1)}, bf16[128,256]{1,0:T(8,128)(2,1)S(1)}, u32[]{:S(2)}, u32[]{:S(2)}) collective-permute-start(bf16[128,256]{1,0:T(8,128)(2,1)S(1)} %constant_dynamic-slice_fusion), channel_id=1, source_target_pairs={{0,16},{16,32},{32,48},{48,64},{64,80},{80,96},{96,112},{112,128},... | collective-permute-start | bytes 196616 | tf_op jit(solution)/shard_map/ppermute | solution.py:29
  22.7 1.9 %collective-permute-done.1 = bf16[128,256]{1,0:T(8,128)(2,1)S(1)} collective-permute-done((bf16[128,256]{1,0:T(8,128)(2,1)S(1)}, bf16[128,256]{1,0:T(8,128)(2,1)S(1)}, u32[]{:S(2)}, u32[]{:S(2)}) %collective-permute-start.1) | collective-permute-done | bytes 65568 | tf_op jit(solution)/shard_map/ppermute | solution.py:29
  24.6 0.1 fusion.54
  24.7 8.9 %all-gather = bf16[256,256]{1,0:T(8,128)(2,1)S(1)} all-gather(bf16[128,256]{1,0:T(8,128)(2,1)S(1)} %fusion.54), channel_id=2, replica_groups=mesh['yl'=4,'zh'=6,'zl'=2,'yh'=2,'x'=4,'core'=2] {'yh'}, dimensions={0}, use_global_device_ids=true | all-gather | bytes 196608 | tf_op jit(solution)/shard_map/all_gather | solution.py:237
  33.6 14.6 %all_to_all.15.own_ref = bf16[4,2,128,256]{3,2,1,0:T(8,128)(2,1)S(1)} all-to-all(bf16[4,2,128,256]{3,2,1,0:T(8,128)(2,1)S(1)} %broadcast_in_dim.64), channel_id=1, replica_groups=mesh['yl'=4,'zh'=6,'zl'=2,'yh'=2,'x'=4,'core'=2] {'x'}, dimensions={0} | all-to-all | bytes 1048576 | tf_op jit(solution)/shard_map/all_to_all | solution.py:191
  48.1 1.9 %collective-permute-start.2 = (bf16[4,2,128,256]{3,2,1,0:T(8,128)(2,1)S(1)}, bf16[4,2,128,256]{3,2,1,0:T(8,128)(2,1)S(1)}, u32[]{:S(2)}, u32[]{:S(2)}) collective-permute-start(bf16[4,2,128,256]{3,2,1,0:T(8,128)(2,1)S(1)} %all_to_all.15.own_ref), channel_id=1, source_target_pairs={{0,1},{1,0},{2,3},{3,2},{4,5},{5,4},{6,7},{7,6},{8,9},{9,8},{10,11... | collective-permute-start | bytes 1572872 | tf_op jit(solution)/shard_map/ppermute | solution.py:239
  50.1 0.0 copy-start.1
  50.1 3.9 %copy.11 = bf16[512,8,2,384]{3,1,2,0:T(8,128)(2,1)S(1)} copy(bf16[512,8,2,384]{3,2,1,0:T(2,128)(2,1)} %bitcast.111) | data formatting | bytes 12582912
  54.0 0.1 pad_add_fusion.pos_ref
  54.0 0.0 collective-permute-done.2.other_ref
  54.0 0.0 copy-done.1
  54.0 1.7 %project.1 = bf16[128,768]{1,0:T(8,128)(2,1)S(1)} custom-call(s32[3]{0:T(128)S(1)} %pad_add_fusion.pos_ref, bf16[4,2,128,256]{3,2,1,0:T(8,128)(2,1)S(1)} %all_to_all.15.own_ref, bf16[4,2,128,256]{3,2,1,0:T(8,128)(2,1)S(1)} %collective-permute-done.2.other_ref, f32[1,4096]{1,0:T(1,128)S(1)} %bitcast.110, bf16[4096,768]{1,0:T(8,128)(2,1)S(1)} %bitcast.109), custom_call_target="tpu_custom_call" | custom-call | flops 805306368 | bytes 8388608 | tf_op jit(solution)/shard_map/project/pallas_call | solution.py:240
  55.8 4.0 %collective-permute-start.3 = (bf16[128,256]{1,0:T(8,128)(2,1)S(1)}, bf16[128,256]{1,0:T(8,128)(2,1)S(1)}, u32[]{:S(2)}, u32[]{:S(2)}) collective-permute-start(bf16[128,256]{1,0:T(8,128)(2,1)S(1)} %broadcast_select_fusion.2), channel_id=1, source_target_pairs={{0,16},{16,0},{1,17},{17,1},{2,18},{18,2},{3,19},{19,3},{4,20},{20... | collective-permute-start | bytes 196616 | tf_op jit(solution)/shard_map/ppermute | solution.py:253
  59.8 0.7 broadcast_in_dim.65
  60.5 13.3 %all-to-all-start.1 = ((bf16[8,128,128]{2,1,0:T(8,128)(2,1)}), bf16[8,128,128]{2,1,0:T(8,128)(2,1)S(1)}, u32[]{:S(2)}, u32[]{:S(2)}) async-start(bf16[8,128,128]{2,1,0:T(8,128)(2,1)} %bitcast.36), calls=%async_computation.1 | async-start | bytes 524288 | tf_op jit(solution)/shard_map/all_to_all | solution.py:191
  73.8 0.0 collective-permute-done.3
  73.9 24.1 %all_gather.11.kv_ref = bf16[1536,256]{1,0:T(8,128)(2,1)S(1)} all-gather(bf16[256,256]{1,0:T(8,128)(2,1)S(1)} %pad_maximum_fusion.1), channel_id=1, replica_groups=mesh['yl'=4,'zh'=6,'zl'=2,'yh'=2,'x'=4,'core'=2] {'zh'}, dimensions={0}, use_global_device_ids=true | all-gather | bytes 917504 | tf_op jit(solution)/shard_map/all_gather | solution.py:261
  98.0 0.0 all-to-all-done.1.q_ref
  98.0 4.8 %attend.1 = bf16[8,144,128]{2,1,0:T(8,128)(2,1)S(1)} custom-call(s32[3]{0:T(128)S(1)} %pad_add_fusion.pos_ref, bf16[8,128,128]{2,1,0:T(8,128)(2,1)S(1)} %all-to-all-done.1.q_ref, bf16[1536,256]{1,0:T(8,128)(2,1)S(1)} %all_gather.11.kv_ref), custom_call_target="tpu_custom_call" | custom-call | tf_op jit(solution)/shard_map/attend/pallas_call | solution.py:263
  102.8 13.6 %all_to_all.16.parts_ref = bf16[8,144,128]{2,1,0:T(8,128)(2,1)} all-to-all(bf16[8,144,128]{2,1,0:T(8,128)(2,1)S(1)} %attend.1), channel_id=1, replica_groups=mesh['yl'=4,'zh'=6,'zl'=2,'yh'=2,'x'=4,'core'=2] {'yl','zl'}, dimensions={0} | all-to-all | bytes 589824 | tf_op jit(solution)/shard_map/all_to_all | solution.py:191
  116.4 1.7 %merge.1 = bf16[128,256]{1,0:T(8,128)(2,1)} custom-call(bf16[8,144,128]{2,1,0:T(8,128)(2,1)} %all_to_all.16.parts_ref), custom_call_target="tpu_custom_call" | custom-call | tf_op jit(solution)/shard_map/merge/pallas_call | solution.py:276
  (17 shorter events, 0.2 us)
Async XLA Ops:
  0.0 2.2 %copy-start = (bf16[1024,1,192]{0,2,1:T(8,128)(2,1)S(1)}, bf16[1024,1,192]{0,2,1:T(8,128)(2,1)}, u32[]{:S(2)}) copy-start(bf16[1024,1,192]{0,2,1:T(8,128)(2,1)} %param.10) | copy-start | bytes 1179652
  0.0 2.4 %copy-start.2 = (bf16[1024,1024]{1,0:T(8,128)(2,1)S(1)}, bf16[1024,1024]{1,0:T(8,128)(2,1)}, u32[]{:S(2)}) copy-start(bf16[1024,1024]{1,0:T(8,128)(2,1)} %param.8) | copy-start | bytes 6291460
  0.0 2.4 %copy-start.6 = (f32[1024]{0:T(1024)S(1)}, f32[1024]{0:T(1024)}, u32[]{:S(2)}) copy-start(f32[1024]{0:T(1024)} %param.9) | copy-start | bytes 12292
  3.3 4.8 %copy-start.5 = (s32[1024]{0:T(1024)S(1)}, s32[1024]{0:T(1024)}, u32[]{:S(2)}) copy-start(s32[1024]{0:T(1024)} %param.13) | copy-start | bytes 12292
  3.3 8.2 %collective-permute-start = (bf16[512,1,128]{0,2,1:T(8,128)(2,1)S(1)}, bf16[512,1,128]{0,2,1:T(8,128)(2,1)S(1)}, u32[]{:S(2)}, u32[]{:S(2)}) collective-permute-start(bf16[512,1,128]{0,2,1:T(8,128)(2,1)S(1)} %slice.69), channel_id=1, source_target_pairs={{0,16},{16,32},{32,48},{48,64},{64,80},{80,96},{96,112},{112,128},... | collective-permute-start | bytes 393224 | tf_op jit(solution)/shard_map/ppermute | solution.py:29
  15.4 1.2 copy-start.3
  17.4 0.8 copy-start.4
  18.4 6.2 %collective-permute-start.1 = (bf16[128,256]{1,0:T(8,128)(2,1)S(1)}, bf16[128,256]{1,0:T(8,128)(2,1)S(1)}, u32[]{:S(2)}, u32[]{:S(2)}) collective-permute-start(bf16[128,256]{1,0:T(8,128)(2,1)S(1)} %constant_dynamic-slice_fusion), channel_id=1, source_target_pairs={{0,16},{16,32},{32,48},{48,64},{64,80},{80,96},{96,112},{112,128},... | collective-permute-start | bytes 196616 | tf_op jit(solution)/shard_map/ppermute | solution.py:29
  48.1 5.9 %collective-permute-start.2 = (bf16[4,2,128,256]{3,2,1,0:T(8,128)(2,1)S(1)}, bf16[4,2,128,256]{3,2,1,0:T(8,128)(2,1)S(1)}, u32[]{:S(2)}, u32[]{:S(2)}) collective-permute-start(bf16[4,2,128,256]{3,2,1,0:T(8,128)(2,1)S(1)} %all_to_all.15.own_ref), channel_id=1, source_target_pairs={{0,1},{1,0},{2,3},{3,2},{4,5},{5,4},{6,7},{7,6},{8,9},{9,8},{10,11... | collective-permute-start | bytes 1572872 | tf_op jit(solution)/shard_map/ppermute | solution.py:239
  50.1 4.0 %copy-start.1 = (f32[4096]{0:T(1024)S(1)}, f32[4096]{0:T(1024)}, u32[]{:S(2)}) copy-start(f32[4096]{0:T(1024)} %param.14) | copy-start | bytes 49156
  55.8 18.0 %collective-permute-start.3 = (bf16[128,256]{1,0:T(8,128)(2,1)S(1)}, bf16[128,256]{1,0:T(8,128)(2,1)S(1)}, u32[]{:S(2)}, u32[]{:S(2)}) collective-permute-start(bf16[128,256]{1,0:T(8,128)(2,1)S(1)} %broadcast_select_fusion.2), channel_id=1, source_target_pairs={{0,16},{16,0},{1,17},{17,1},{2,18},{18,2},{3,19},{19,3},{4,20},{20... | collective-permute-start | bytes 196616 | tf_op jit(solution)/shard_map/ppermute | solution.py:253
  60.5 37.5 %all-to-all-start.1 = ((bf16[8,128,128]{2,1,0:T(8,128)(2,1)}), bf16[8,128,128]{2,1,0:T(8,128)(2,1)S(1)}, u32[]{:S(2)}, u32[]{:S(2)}) async-start(bf16[8,128,128]{2,1,0:T(8,128)(2,1)} %bitcast.36), calls=%async_computation.1 | async-start | bytes 524288 | tf_op jit(solution)/shard_map/all_to_all | solution.py:191

commit v2 on v1

v2 whole, which is shorter than its diff:
```python
import functools
import math

import jax
import jax.numpy as jnp
from jax import lax
from jax.experimental import pallas as pl
from jax.experimental.pallas import tpu as pltpu
from jax.sharding import Mesh, PartitionSpec as P

CTX = ("yl", "zh", "zl")
HEAD = ("yh", "x", "core")
Y_LO, Z_HALF, Z_PAIR, Y_HI, X, CORE = 4, 6, 2, 2, 4, 2
N_CTX = Y_LO * Z_HALF * Z_PAIR

DH_L = 64
DH = 128
PATCH_LEN = 8
DG = 4096


neg_large = -1e30


def passed_along(block, axis, distance):
    devices = range(N_CTX)
    route = [(i - distance, i) for i in devices if i - distance in devices]
    return lax.ppermute(block, axis, route)


def rows_arriving(states_ref, held_ref, sems, first_row):
    step = held_ref.shape[1]
    copies = []
    for part in range(held_ref.shape[0]):
        rows = pl.ds(first_row + part * step, step)
        copy = pltpu.make_async_copy(states_ref.at[rows], held_ref.at[part], sems.at[part])
        copy.start()
        copies.append(copy)
    return copies


def norm_rows(states_ref, gain_ref, normed_ref):
    step = 32
    gain = gain_ref[...]
    for first in range(0, states_ref.shape[0], step):
        states = states_ref[first : first + step].astype(jnp.float32)
        scale = lax.rsqrt(jnp.mean(states * states, axis=1, keepdims=True) + 1e-05)
        normed_ref[first : first + step] = (states * scale * gain).astype(jnp.bfloat16)


def project_rows(weight_ref, normed_ref):
    return lax.dot_general(
        weight_ref[...], normed_ref[...], (((1,), (1,)), ((), ())), preferred_element_type=jnp.float32
    ).astype(jnp.bfloat16)


def second_half_kernel(
    states_ref, gain_hbm, w_hbm, query_ref, rim_ref, held_ref, normed_ref, gain_ref, w_ref, sems
):
    half = query_ref.shape[1]
    parts = held_ref.shape[0]
    gain_copy = pltpu.make_async_copy(gain_hbm, gain_ref, sems.at[parts])
    gain_copy.start()
    copies = rows_arriving(states_ref, held_ref, sems, half)
    w_copy = pltpu.make_async_copy(w_hbm, w_ref, sems.at[parts + 1])
    w_copy.start()
    gain_copy.wait()
    step = held_ref.shape[1]
    for part, copy in enumerate(copies):
        copy.wait()
        norm_rows(held_ref.at[part], gain_ref, normed_ref.at[pl.ds(part * step, step)])
    w_copy.wait()
    proj = project_rows(w_ref, normed_ref)
    query_ref[...] = proj[:DH_L]
    rim_ref[...] = proj[DH_L:]


def window_attend(queries_t, keys_ref, values_ref, early_bias, out_ref):
    scale = 1.0 / math.sqrt(DH_L)
    width = 128
    blocks = range(queries_t.shape[1] // width)
    row_at = lax.broadcasted_iota(jnp.int32, (width, width), 0)
    col_at = lax.broadcasted_iota(jnp.int32, (width, width), 1)
    scores = []
    for block in blocks:
        block_scores = []
        queries = queries_t[:, block * width : (block + 1) * width]
        for part in range(5):
            at = (block + part) * width
            part_scores = jnp.dot(
                keys_ref[at : at + width], queries, preferred_element_type=jnp.float32
            )
            if part == 0:
                part_scores = jnp.where(row_at > col_at, part_scores, neg_large)
            if part == 4:
                part_scores = jnp.where(row_at <= col_at, part_scores, neg_large)
            if early_bias is not None and at < keys_ref.shape[0] // 2:
                part_scores = part_scores + early_bias
            block_scores.append(part_scores)
        scores.append(block_scores)
    weights = []
    normalizers = []
    for block in blocks:
        peak = jnp.max(functools.reduce(jnp.maximum, scores[block]), axis=0, keepdims=True)
        block_weights = [jnp.exp((part_scores - peak) * scale) for part_scores in scores[block]]
        normalizers.append(
            jnp.sum(functools.reduce(jnp.add, block_weights), axis=0, keepdims=True)
        )
        weights.append(
            jnp.concatenate([part.astype(jnp.bfloat16) for part in block_weights], axis=0)
        )
    summed = [
        jnp.dot(
            values_ref[:, block * width : (block + 5) * width],
            weights[block],
            preferred_element_type=jnp.float32,
        )
        for block in blocks
    ]
    for block in blocks:
        out_ref[block * width : (block + 1) * width] = (
            summed[block] / normalizers[block]
        ).T.astype(jnp.bfloat16)


def started(pairs, sems, first):
    copies = [
        pltpu.make_async_copy(source, target, sems.at[first + at])
        for at, (source, target) in enumerate(pairs)
    ]
    for copy in copies:
        copy.start()
    return copies


def first_half_kernel(
    states_ref, gain_hbm, w_hbm, query_hbm, second_hbm, first_ref, out_ref,
    held_ref, normed_ref, gain_ref, w_ref, query_ref, second_ref, keys_ref, values_ref, sems,
):
    half = first_ref.shape[1]
    parts = held_ref.shape[0]
    step = held_ref.shape[1]
    (gain_copy,) = started(((gain_hbm, gain_ref),), sems, parts)
    copies = rows_arriving(states_ref, held_ref, sems, 0)
    others = started(
        ((second_hbm, second_ref), (w_hbm, w_ref), (query_hbm, query_ref)), sems, parts + 1
    )
    gain_copy.wait()
    for part, copy in enumerate(copies):
        copy.wait()
        norm_rows(held_ref.at[part], gain_ref, normed_ref.at[pl.ds(part * step, step)])
    for copy in others:
        copy.wait()
    keys_ref[half:] = second_ref[:DH_L].T
    values_ref[:, half:] = second_ref[DH_L:]
    proj = project_rows(w_ref, normed_ref)
    first_ref[...] = proj
    keys_ref[:half] = proj[DH_L : 2 * DH_L].T
    values_ref[:, :half] = proj[2 * DH_L :]
    window_attend(query_ref[...], keys_ref, values_ref, None, out_ref)


def patch_kernel(
    rim_hbm, first_hbm, late_hbm, patch_hbm, cross_hbm, lift_hbm, kept_ref, leaving_ref,
    rim_ref, first_ref, patch_ref, cross_ref, lift_ref, keys_ref, values_ref, local_ref, sems,
):
    ctx = lax.axis_index(CTX)
    half = first_ref.shape[1]
    copies = started(
        (
            (rim_hbm, rim_ref),
            (first_hbm, first_ref),
            (late_hbm, local_ref.at[pl.ds(half, half)]),
            (patch_hbm, patch_ref),
            (cross_hbm, cross_ref),
            (lift_hbm, lift_ref),
        ),
        sems,
        0,
    )
    for copy in copies:
        copy.wait()
    rim_bias = jnp.where(ctx > 0, 0.0, neg_large).astype(jnp.float32)
    keys_ref[:half] = rim_ref[:DH_L].T
    keys_ref[half:] = first_ref[DH_L : 2 * DH_L].T
    values_ref[:, :half] = rim_ref[DH_L:]
    values_ref[:, half:] = first_ref[2 * DH_L :]
    window_attend(first_ref[:DH_L], keys_ref, values_ref, rim_bias, local_ref)
    local_out = local_ref[...]
    quota = kept_ref.shape[0]
    slots = 2 * quota
    slot_of = patch_ref[...] - ctx * quota
    member = slot_of == lax.broadcasted_iota(jnp.int32, (slots, 2 * half), 0)
    member_f = jnp.where(member, 1.0, 0.0)
    counts = jnp.sum(member_f, axis=1, keepdims=True)
    pooled = (
        jnp.dot(member_f.astype(jnp.bfloat16), local_out, preferred_element_type=jnp.float32)
        / jnp.maximum(counts, 1.0)
    ).astype(jnp.bfloat16)
    keys = jnp.dot(
        local_out, cross_ref[:, :DH_L], preferred_element_type=jnp.float32
    ).astype(jnp.bfloat16)
    values = jnp.dot(
        local_out, cross_ref[:, DH_L:], preferred_element_type=jnp.float32
    ).astype(jnp.bfloat16)
    scores = lax.dot_general(
        pooled, keys, (((1,), (1,)), ((), ())), preferred_element_type=jnp.float32
    )
    scores = jnp.where(member, scores, neg_large)
    peak = jnp.max(scores, axis=1, keepdims=True)
    weights = jnp.where(member, jnp.exp((scores - peak) * (1.0 / math.sqrt(DH_L))), 0.0)
    normalizer = jnp.sum(weights, axis=1, keepdims=True)
    normalizer = jnp.where(normalizer > 0, normalizer, 1.0)
    attended = jnp.dot(
        weights.astype(jnp.bfloat16), values, preferred_element_type=jnp.float32
    ) / normalizer
    lifted = jnp.dot(pooled, lift_ref[...], preferred_element_type=jnp.float32)
    patch_rows = (lifted + attended).astype(jnp.bfloat16)
    kept_ref[...] = patch_rows[:quota]
    leaving_ref[...] = patch_rows[quota:]


def project_kernel(
    own_ref, other_ref, gain_ref, w_ref, queries_ref, keep_ref, send_ref, scaled_ref
):
    core = lax.axis_index("core")
    zl = lax.axis_index("zl")
    rows = own_ref.shape[2]
    width = own_ref.shape[3]
    squares = jnp.zeros((rows, 128), jnp.float32)
    for block_ref, block_core in ((own_ref, core), (other_ref, 1 - core)):
        for x in range(X):
            for yh in range(Y_HI):
                block = block_ref[x, yh].astype(jnp.float32)
                first = pl.multiple_of((yh * X * CORE + x * CORE + block_core) * width, width)
                gain = gain_ref[:, pl.ds(first, width)]
                for lanes in range(0, width, 128):
                    piece = block[:, lanes : lanes + 128]
                    squares = squares + piece * piece
                scaled_ref[:, pl.ds(first, width)] = (block * gain).astype(jnp.bfloat16)
    total = jnp.dot(scaled_ref[...], w_ref[...], preferred_element_type=jnp.float32)
    row_scale = lax.rsqrt(jnp.sum(squares, axis=1, keepdims=True) / DG + 1e-05)
    total = (total * row_scale).astype(jnp.bfloat16)
    for head in range(2):
        queries = total[:, head * 3 * DH : head * 3 * DH + DH]
        for yy in range(Y_LO):
            queries_ref[2 * yy + head] = queries
        keys_vals = total[:, head * 3 * DH + DH : (head + 1) * 3 * DH]

        @pl.when(zl == head)
        def _():
            keep_ref[...] = keys_vals

        @pl.when(zl != head)
        def _():
            send_ref[...] = keys_vals


def attend_kernel(q_ref, kv_ref, out_ref, vt_ref, s_ref):
    y = lax.axis_index("yl")
    zh = lax.axis_index("zh")
    key_count = kv_ref.shape[0]
    rows = 2 * q_ref.shape[1]
    half = q_ref.shape[1]
    scale = 1.0 / math.sqrt(DH)
    vt_ref[...] = kv_ref[:, DH:].T
    chunk = 256

    def attend(yy, masked):
        queries = q_ref[pl.ds(2 * yy, 2)].reshape(rows, DH)
        peak = jnp.full((1, rows), neg_large, jnp.float32)
        for first in range(0, key_count, chunk):
            scores = lax.dot_general(
                kv_ref[first : first + chunk, :DH],
                queries,
                (((1,), (1,)), ((), ())),
                preferred_element_type=jnp.float32,
            )
            if masked:
                key_at = first + lax.broadcasted_iota(jnp.int32, scores.shape, 0)
                query_at = zh * rows + lax.broadcasted_iota(jnp.int32, scores.shape, 1)
                scores = jnp.where(key_at <= query_at, scores, neg_large)
            s_ref[first : first + chunk] = scores
            peak = jnp.maximum(peak, jnp.max(scores, axis=0, keepdims=True))
        normalizer = jnp.zeros((1, rows), jnp.float32)
        summed = jnp.zeros((DH, rows), jnp.float32)
        for first in range(0, key_count, chunk):
            weights = jnp.exp((s_ref[first : first + chunk] - peak) * scale)
            normalizer = normalizer + jnp.sum(weights, axis=0, keepdims=True)
            summed = summed + jnp.dot(
                vt_ref[:, first : first + chunk],
                weights.astype(jnp.bfloat16),
                preferred_element_type=jnp.float32,
            )
        summed = (summed / normalizer).astype(jnp.bfloat16)
        level = peak * scale + jnp.log(normalizer)
        high = level.astype(jnp.bfloat16)
        rest = level - high.astype(jnp.float32)
        mid = rest.astype(jnp.bfloat16)
        low = (rest - mid.astype(jnp.float32)).astype(jnp.bfloat16)
        stats = jnp.concatenate(
            [high, mid, low, jnp.zeros((13, rows), jnp.bfloat16)], axis=0
        )
        for part in range(2):
            lanes = slice(part * half, (part + 1) * half)
            out_ref[2 * yy + part, :DH, :] = summed[:, lanes]
            out_ref[2 * yy + part, DH:, :] = stats[:, lanes]

    for yy in range(Y_LO):

        @pl.when(yy < y)
        def _():
            row_at = lax.broadcasted_iota(jnp.int32, (16, half), 0)
            stats = jnp.where(row_at == 0, neg_large, 0.0).astype(jnp.bfloat16)
            for part in range(2):
                out_ref[2 * yy + part, :DH, :] = jnp.zeros((DH, half), jnp.bfloat16)
                out_ref[2 * yy + part, DH:, :] = stats

        @pl.when(yy == y)
        def _():
            attend(yy, True)

        @pl.when(yy > y)
        def _():
            attend(yy, False)


def merge_kernel(parts_ref, out_ref):
    for head in range(2):
        levels = []
        for yy in range(Y_LO):
            stats = parts_ref[2 * yy + head, DH:, :].astype(jnp.float32)
            levels.append(stats[0:1] + stats[1:2] + stats[2:3])
        peak = functools.reduce(jnp.maximum, levels)
        total = jnp.zeros((DH, out_ref.shape[0]), jnp.float32)
        normalizer = jnp.zeros((1, out_ref.shape[0]), jnp.float32)
        for yy in range(Y_LO):
            share = jnp.exp(levels[yy] - peak)
            normalizer = normalizer + share
            total = total + share * parts_ref[2 * yy + head, :DH, :].astype(jnp.float32)
        out_ref[:, head * DH : (head + 1) * DH] = (total / normalizer).T.astype(jnp.bfloat16)


VMEM = pl.BlockSpec(memory_space=pltpu.VMEM)


def all_to_all_of(block, axes):
    return lax.all_to_all(block, axes, 0, 0, tiled=True)


def local(enc_states, local_gain, w_local, w_cross, w_patch, byte_patch, global_gain, w_global):
    byte_count = enc_states.shape[0]
    quota = byte_count // PATCH_LEN
    half = byte_count // 2
    zl = lax.axis_index("zl")
    w_rows = jnp.transpose(w_local.reshape(w_local.shape[0], 3 * DH_L))
    model = enc_states.shape[1]
    HBM = pl.BlockSpec(memory_space=pltpu.HBM)
    held = [
        pltpu.VMEM((4, half // 4, model), jnp.bfloat16),
        pltpu.VMEM((half, model), jnp.bfloat16),
        pltpu.VMEM((1, model), jnp.float32),
        pltpu.VMEM((3 * DH_L, model), jnp.bfloat16),
    ]
    window_scratch = [
        pltpu.VMEM((byte_count, DH_L), jnp.bfloat16),
        pltpu.VMEM((DH_L, byte_count), jnp.bfloat16),
    ]
    gain_row = local_gain.reshape(1, -1)
    rim_shape = (2 * DH_L, half)
    late_queries, rim_sent = pl.pallas_call(
        second_half_kernel,
        out_shape=[
            jax.ShapeDtypeStruct((DH_L, half), jnp.bfloat16),
            jax.ShapeDtypeStruct(rim_shape, jnp.bfloat16),
        ],
        in_specs=[HBM] * 3,
        out_specs=[VMEM] * 2,
        scratch_shapes=held + [pltpu.SemaphoreType.DMA((6,))],
        compiler_params=pltpu.CompilerParams(vmem_limit_bytes=59 << 20),
        name="second_half",
    )(enc_states, gain_row, w_rows)
    rim = passed_along(rim_sent, CTX, 1)
    first_proj, late_out = pl.pallas_call(
        first_half_kernel,
        out_shape=[
            jax.ShapeDtypeStruct((3 * DH_L, half), jnp.bfloat16),
            jax.ShapeDtypeStruct((half, DH_L), jnp.bfloat16),
        ],
        in_specs=[HBM] * 5,
        out_specs=[VMEM] * 2,
        scratch_shapes=held
        + [pltpu.VMEM((DH_L, half), jnp.bfloat16), pltpu.VMEM(rim_shape, jnp.bfloat16)]
        + window_scratch
        + [pltpu.SemaphoreType.DMA((8,))],
        compiler_params=pltpu.CompilerParams(vmem_limit_bytes=59 << 20),
        cost_estimate=pl.CostEstimate(
            flops=2 * half * byte_count * 3 * DH_L + 4 * half * byte_count * DH_L,
            bytes_accessed=8 << 20,
            transcendentals=half * byte_count,
        ),
        name="first_half",
    )(enc_states, gain_row, w_rows, late_queries, rim_sent)
    kept_rows, leaving = pl.pallas_call(
        patch_kernel,
        out_shape=[jax.ShapeDtypeStruct((quota, w_patch.shape[2]), jnp.bfloat16)] * 2,
        in_specs=[HBM] * 6,
        out_specs=[VMEM, VMEM],
        scratch_shapes=[
            pltpu.VMEM(rim_shape, jnp.bfloat16),
            pltpu.VMEM((3 * DH_L, half), jnp.bfloat16),
            pltpu.VMEM((1, byte_count), jnp.int32),
            pltpu.VMEM(w_cross.shape[1:], jnp.bfloat16),
            pltpu.VMEM(w_patch.shape[1:], jnp.bfloat16),
        ]
        + window_scratch
        + [pltpu.VMEM((byte_count, DH_L), jnp.bfloat16), pltpu.SemaphoreType.DMA((6,))],
        compiler_params=pltpu.CompilerParams(vmem_limit_bytes=59 << 20),
        name="patches",
    )(rim, first_proj, late_out, byte_patch.reshape(1, -1), w_cross[0], w_patch[0])
    slab_rows = kept_rows + passed_along(leaving, CTX, 1)
    head_total = w_global.shape[1]
    flat_weight = w_global.reshape(DG, head_total * 3 * DH)
    slab_rows, flat_weight = lax.optimization_barrier((slab_rows, flat_weight))
    pair_rows = lax.all_gather(slab_rows, "yh", axis=0)
    own_rows = all_to_all_of(jnp.broadcast_to(pair_rows[None], (X,) + pair_rows.shape), "x")
    other_rows = lax.ppermute(own_rows, "core", [(0, 1), (1, 0)])
    queries, kept_kv, sent_kv = pl.pallas_call(
        project_kernel,
        out_shape=[
            jax.ShapeDtypeStruct((Y_LO * Z_PAIR, quota, DH), jnp.bfloat16),
            jax.ShapeDtypeStruct((quota, 2 * DH), jnp.bfloat16),
            jax.ShapeDtypeStruct((quota, 2 * DH), jnp.bfloat16),
        ],
        in_specs=[VMEM] * 4,
        out_specs=[VMEM, VMEM, VMEM],
        scratch_shapes=[pltpu.VMEM((quota, DG), jnp.bfloat16)],
        compiler_params=pltpu.CompilerParams(vmem_limit_bytes=32 << 20),
        cost_estimate=pl.CostEstimate(
            flops=2 * quota * DG * head_total * 3 * DH, bytes_accessed=8 << 20, transcendentals=0
        ),
        name="project",
    )(own_rows, other_rows, global_gain.reshape(1, DG), flat_weight)
    swapped = lax.ppermute(sent_kv, "zl", [(0, 1), (1, 0)])
    queries = all_to_all_of(queries, ("yl", "zl"))
    pair_kv = jnp.concatenate(
        [jnp.where(zl == 0, kept_kv, swapped), jnp.where(zl == 0, swapped, kept_kv)], axis=0
    )
    keys_vals = lax.all_gather(pair_kv, "zh", axis=0, tiled=True)
    key_count = keys_vals.shape[0]
    partial_out = pl.pallas_call(
        attend_kernel,
        out_shape=jax.ShapeDtypeStruct((Y_LO * Z_PAIR, DH + 16, quota), jnp.bfloat16),
        in_specs=[VMEM, VMEM],
        out_specs=VMEM,
        scratch_shapes=[
            pltpu.VMEM((DH, key_count), jnp.bfloat16),
            pltpu.VMEM((key_count, 2 * quota), jnp.float32),
        ],
        compiler_params=pltpu.CompilerParams(vmem_limit_bytes=32 << 20),
        name="attend",
    )(queries, keys_vals)
    parts = all_to_all_of(partial_out, ("yl", "zl"))
    return pl.pallas_call(
        merge_kernel,
        out_shape=jax.ShapeDtypeStruct((quota, head_total * DH), jnp.bfloat16),
        in_specs=[VMEM],
        out_specs=VMEM,
        compiler_params=pltpu.CompilerParams(vmem_limit_bytes=8 << 20),
        name="merge",
    )(parts)


def solution(mesh):
    split = Mesh(
        mesh.devices.reshape(Y_LO, Z_HALF, Z_PAIR, Y_HI, X, CORE), CTX + HEAD
    )
    in_specs = (
        P(CTX, None),
        P(),
        P(None, HEAD, None),
        P(HEAD, None, None),
        P(HEAD, None, None),
        P(CTX),
        P(),
        P(None, HEAD, None),
    )
    out_specs = P(CTX, HEAD)
    return jax.shard_map(local, mesh=split, in_specs=in_specs, out_specs=out_specs, check_vma=False)
```

time: 119 us -> 112 us (0.941)
  Pallas kernels: 8.26 us -> 18.1 us
  matrix products: 5.81 us -> 0 us
  other arithmetic: 5.61 us -> 0.05 us
  starting transfers between devices: 27.7 us -> 25.1 us
  between operations: 2.27 us -> 0.15 us
    pallas_call x1 -> x4, Pallas kernels: 1.7 us -> 12.7 us  [the longest x1 4.09 us: local(): pl.pallas_call(patch_kernel, out_shape=[jax.ShapeDtypeStruct((quota, w_pa...]
    dot_general x10 -> x0, matrix products: 5.81 us -> none  [the longest x3 2.06 us: masked_softmax_apply(): jnp.einsum('hqk,khd->qhd', weights.astype(jnp.bfloat16), values, preferre...]
    reduce_sum x4 -> x0, other arithmetic: 4.72 us -> none  [the longest x2 2.31 us: masked_softmax_apply(): normalizer = jnp.sum(weights, axis=-1)]
    ppermute x1, starting transfers between devices: 3.96 us -> 1.91 us  [local(): swapped = lax.ppermute(sent_kv, 'zl', [(0, 1), (1, 0)])]
    all_gather x1, blocking collectives: 24.1 us -> 26 us  [local(): keys_vals = lax.all_gather(pair_kv, 'zh', axis=0, tiled=True)]
    ppermute x1, waiting for transfers between devices: 0.01 us -> 1.88 us  [local(): other_rows = lax.ppermute(own_rows, 'core', [(0, 1), (1, 0)])]
    ppermute x2, waiting for transfers between devices: 1.88 us -> 0.01 us  [passed_along(): return lax.ppermute(block, axis, route)]
    all_to_all x2, blocking collectives: 28.1 us -> 26.4 us  [all_to_all_of(): return lax.all_to_all(block, axes, 0, 0, tiled=True)]
  transfers between devices with their start and end apart: 5 -> 5, of which waited for: 1 -> 1; matrix products, arithmetic and copies ran while one was open for 6% -> 4% of each run, Pallas kernels for 0% -> 3%
where the time goes in v2:
time: 112 us; the launch traced here: 111 us
  blocking collectives  61.3 us (55%)
  starting transfers between devices  25.1 us (22%)
  Pallas kernels  18.1 us (16%)
  local copies, waits for them, and re-layouts  4.59 us (4%)
  waiting for transfers between devices  1.89 us (2%)
    all_to_all x2, blocking collectives, all_to_all_of(): return lax.all_to_all(block, axes, 0, 0, tiled=True)  26.4 us
    all_gather x1, blocking collectives, local(): keys_vals = lax.all_gather(pair_kv, 'zh', axis=0, tiled=True)  26 us
    all_to_all x1, starting transfers between devices, all_to_all_of(): return lax.all_to_all(block, axes, 0, 0, tiled=True)  12.8 us
    all_gather x1, blocking collectives, local(): pair_rows = lax.all_gather(slab_rows, 'yh', axis=0)  8.85 us
    ppermute x2, starting transfers between devices, passed_along(): return lax.ppermute(block, axis, route)  8.55 us
    pallas_call x1, Pallas kernels, local(): pl.pallas_call(attend_kernel, out_shape=jax.ShapeDtypeStruct((Y_LO * Z_PA...  4.66 us
    unnamed x7, local copies, waits for them, and re-layouts  4.56 us
    pallas_call x1, Pallas kernels, local(): pl.pallas_call(patch_kernel, out_shape=[jax.ShapeDtypeStruct((quota, w_pa...  4.09 us
  transfers between devices with their start and end apart: 5, of which 1 were waited for; matrix products, arithmetic and copies ran while one was open for 4% of the time, Pallas kernels for 3%

profile of v2, /device:TPU:2, one launch (start us, length us, event | category | flops | bytes accessed | tf_op | source)
XLA Modules:
  0.0 111.2 jit_solution(14456039230614313757)
XLA Ops:
  0.0 2.8 %second_half.1 = (bf16[64,512]{1,0:T(8,128)(2,1)}, bf16[128,512]{1,0:T(8,128)(2,1)}) custom-call(bf16[1024,1024]{1,0:T(8,128)(2,1)} %states_ref.3, f32[1,1024]{1,0:T(1,128)} %bitcast.19, bf16[192,1024]{1,0:T(8,128)(2,1)} %bitcast.14), custom_call_target="tpu_custom_call" | custom-call | tf_op jit(solution)/shard_map/second_half/pallas_call | solution.py:371
  2.8 4.3 %collective-permute-start = (bf16[128,512]{1,0:T(8,128)(2,1)}, bf16[128,512]{1,0:T(8,128)(2,1)S(1)}, u32[]{:S(2)}, u32[]{:S(2)}) collective-permute-start(bf16[128,512]{1,0:T(8,128)(2,1)} %get-tuple-element.16.second_hbm), channel_id=1, source_target_pairs={{0,16},{16,32},{32,48},{48,64},{64,80},{80,96},{96,112},{112,128},... | collective-permute-start | bytes 393224 | tf_op jit(solution)/shard_map/ppermute | solution.py:28
  7.1 3.7 %first_half.1 = (bf16[192,512]{1,0:T(8,128)(2,1)}, bf16[512,64]{1,0:T(8,128)(2,1)}) custom-call(bf16[1024,1024]{1,0:T(8,128)(2,1)} %states_ref.3, f32[1,1024]{1,0:T(1,128)} %bitcast.20, bf16[192,1024]{1,0:T(8,128)(2,1)} %bitcast.15, bf16[64,512]{1,0:T(8,128)(2,1)} %get-tuple-element.17.query_hbm, bf16[128,512]{1,0:T(8,128)(2,1)} %get-tuple-element.16.second_hbm), custom_call_target="tpu_custom_call" | custom-call | flops 335544320 | bytes 8388608 | tf_op jit(solution)/shard_map/first_half/pallas_call | solution.py:384
  10.8 0.0 collective-permute-done.rim_hbm
  10.8 0.0 copy-start.1
  10.8 0.6 copy-done.1
  11.5 4.1 %patches.1 = (bf16[128,256]{1,0:T(8,128)(2,1)}, bf16[128,256]{1,0:T(8,128)(2,1)}) custom-call(bf16[128,512]{1,0:T(8,128)(2,1)} %copy-done.1, bf16[192,512]{1,0:T(8,128)(2,1)} %get-tuple-element.18.first_hbm, bf16[512,64]{1,0:T(8,128)(2,1)} %get-tuple-element.19.late_hbm, s32[1,1024]{1,0:T(1,128)} %bitcast.21, bf16[64,320]{1,0:T(8,128)(2,1)} %bitcast.17, ...), custom_call_target="tpu_custom_call" | custom-call | tf_op jit(solution)/shard_map/patches/pallas_call | solution.py:404
  15.6 4.3 %collective-permute-start.1 = (bf16[128,256]{1,0:T(8,128)(2,1)}, bf16[128,256]{1,0:T(8,128)(2,1)S(1)}, u32[]{:S(2)}, u32[]{:S(2)}) collective-permute-start(bf16[128,256]{1,0:T(8,128)(2,1)} %get-tuple-element.21), channel_id=1, source_target_pairs={{0,16},{16,32},{32,48},{48,64},{64,80},{80,96},{96,112},{112,128},... | collective-permute-start | bytes 196616 | tf_op jit(solution)/shard_map/ppermute | solution.py:28
  19.9 0.0 copy-start.2
  19.9 0.0 copy-start
  19.9 3.9 %copy.9 = bf16[512,8,2,384]{3,1,2,0:T(8,128)(2,1)S(1)} copy(bf16[512,8,2,384]{3,2,1,0:T(2,128)(2,1)} %bitcast.13) | data formatting | bytes 12582912
  23.8 0.0 collective-permute-done.1
  23.8 0.0 copy-done.2
  23.8 8.9 %all-gather = bf16[256,256]{1,0:T(8,128)(2,1)S(1)} all-gather(bf16[128,256]{1,0:T(8,128)(2,1)S(1)} %add.3), channel_id=2, replica_groups=mesh['yl'=4,'zh'=6,'zl'=2,'yh'=2,'x'=4,'core'=2] {'yh'}, dimensions={0}, use_global_device_ids=true | all-gather | bytes 196608 | tf_op jit(solution)/shard_map/all_gather | solution.py:425
  32.7 15.7 %all_to_all.15.own_ref = bf16[4,2,128,256]{3,2,1,0:T(8,128)(2,1)S(1)} all-to-all(bf16[4,2,128,256]{3,2,1,0:T(8,128)(2,1)S(1)} %broadcast_in_dim.2), channel_id=1, replica_groups=mesh['yl'=4,'zh'=6,'zl'=2,'yh'=2,'x'=4,'core'=2] {'x'}, dimensions={0} | all-to-all | bytes 1048576 | tf_op jit(solution)/shard_map/all_to_all | solution.py:348
  48.4 1.9 %collective-permute-start.2 = (bf16[4,2,128,256]{3,2,1,0:T(8,128)(2,1)S(1)}, bf16[4,2,128,256]{3,2,1,0:T(8,128)(2,1)S(1)}, u32[]{:S(2)}, u32[]{:S(2)}) collective-permute-start(bf16[4,2,128,256]{3,2,1,0:T(8,128)(2,1)S(1)} %all_to_all.15.own_ref), channel_id=1, source_target_pairs={{0,1},{1,0},{2,3},{3,2},{4,5},{5,4},{6,7},{7,6},{8,9},{9,8},{10,11... | collective-permute-start | bytes 1572872 | tf_op jit(solution)/shard_map/ppermute | solution.py:427
  50.3 1.9 %collective-permute-done.2.other_ref = bf16[4,2,128,256]{3,2,1,0:T(8,128)(2,1)S(1)} collective-permute-done((bf16[4,2,128,256]{3,2,1,0:T(8,128)(2,1)S(1)}, bf16[4,2,128,256]{3,2,1,0:T(8,128)(2,1)S(1)}, u32[]{:S(2)}, u32[]{:S(2)}) %collective-permute-start.2) | collective-permute-done | bytes 524320 | tf_op jit(solution)/shard_map/ppermute | solution.py:427
  52.2 0.0 copy-done
  52.2 2.1 %project.1 = (bf16[8,128,128]{2,1,0:T(8,128)(2,1)}, bf16[128,256]{1,0:T(8,128)(2,1)S(1)}, bf16[128,256]{1,0:T(8,128)(2,1)S(1)}) custom-call(bf16[4,2,128,256]{3,2,1,0:T(8,128)(2,1)S(1)} %all_to_all.15.own_ref, bf16[4,2,128,256]{3,2,1,0:T(8,128)(2,1)S(1)} %collective-permute-done.2.other_ref, f32[1,4096]{1,0:T(1,128)S(1)} %bitcast.12, ...), custom_call_target="tpu_custom_call" | custom-call | flops 805306368 | bytes 8388608 | tf_op jit(solution)/shard_map/project/pallas_call | solution.py:428
  54.3 1.9 %collective-permute-start.3 = (bf16[128,256]{1,0:T(8,128)(2,1)S(1)}, bf16[128,256]{1,0:T(8,128)(2,1)S(1)}, u32[]{:S(2)}, u32[]{:S(2)}) collective-permute-start(bf16[128,256]{1,0:T(8,128)(2,1)S(1)} %get-tuple-element.26), channel_id=1, source_target_pairs={{0,16},{16,0},{1,17},{17,1},{2,18},{18,2},{3,19},{19,3},{4,20},{20... | collective-permute-start | bytes 196616 | tf_op jit(solution)/shard_map/ppermute | solution.py:444
  56.2 12.8 %all-to-all-start.1 = ((bf16[8,128,128]{2,1,0:T(8,128)(2,1)}), bf16[8,128,128]{2,1,0:T(8,128)(2,1)S(1)}, u32[]{:S(2)}, u32[]{:S(2)}) async-start(bf16[8,128,128]{2,1,0:T(8,128)(2,1)} %get-tuple-element.24), calls=%async_computation.1 | async-start | bytes 524288 | tf_op jit(solution)/shard_map/all_to_all | solution.py:348
  69.0 0.0 collective-permute-done.3
  69.1 26.0 %all_gather.11.kv_ref = bf16[1536,256]{1,0:T(8,128)(2,1)S(1)} all-gather(bf16[256,256]{1,0:T(8,128)(2,1)S(1)} %pad_maximum_fusion), channel_id=1, replica_groups=mesh['yl'=4,'zh'=6,'zl'=2,'yh'=2,'x'=4,'core'=2] {'zh'}, dimensions={0}, use_global_device_ids=true | all-gather | bytes 917504 | tf_op jit(solution)/shard_map/all_gather | solution.py:449
  95.1 0.0 all-to-all-done.1.q_ref
  95.1 4.7 %attend.1 = bf16[8,144,128]{2,1,0:T(8,128)(2,1)S(1)} custom-call(bf16[8,128,128]{2,1,0:T(8,128)(2,1)S(1)} %all-to-all-done.1.q_ref, bf16[1536,256]{1,0:T(8,128)(2,1)S(1)} %all_gather.11.kv_ref), custom_call_target="tpu_custom_call" | custom-call | tf_op jit(solution)/shard_map/attend/pallas_call | solution.py:451
  99.8 10.7 %all_to_all.16.parts_ref = bf16[8,144,128]{2,1,0:T(8,128)(2,1)S(1)} all-to-all(bf16[8,144,128]{2,1,0:T(8,128)(2,1)S(1)} %attend.1), channel_id=1, replica_groups=mesh['yl'=4,'zh'=6,'zl'=2,'yh'=2,'x'=4,'core'=2] {'yl','zl'}, dimensions={0} | all-to-all | bytes 589824 | tf_op jit(solution)/shard_map/all_to_all | solution.py:348
  110.4 0.8 merge.1
  (4 shorter events, 0.1 us)
Async XLA Ops:
  2.8 8.0 %collective-permute-start = (bf16[128,512]{1,0:T(8,128)(2,1)}, bf16[128,512]{1,0:T(8,128)(2,1)S(1)}, u32[]{:S(2)}, u32[]{:S(2)}) collective-permute-start(bf16[128,512]{1,0:T(8,128)(2,1)} %get-tuple-element.16.second_hbm), channel_id=1, source_target_pairs={{0,16},{16,32},{32,48},{48,64},{64,80},{80,96},{96,112},{112,128},... | collective-permute-start | bytes 393224 | tf_op jit(solution)/shard_map/ppermute | solution.py:28
  10.8 0.7 copy-start.1
  15.6 8.2 %collective-permute-start.1 = (bf16[128,256]{1,0:T(8,128)(2,1)}, bf16[128,256]{1,0:T(8,128)(2,1)S(1)}, u32[]{:S(2)}, u32[]{:S(2)}) collective-permute-start(bf16[128,256]{1,0:T(8,128)(2,1)} %get-tuple-element.21), channel_id=1, source_target_pairs={{0,16},{16,32},{32,48},{48,64},{64,80},{80,96},{96,112},{112,128},... | collective-permute-start | bytes 196616 | tf_op jit(solution)/shard_map/ppermute | solution.py:28
  19.9 3.9 %copy-start.2 = (bf16[128,256]{1,0:T(8,128)(2,1)S(1)}, bf16[128,256]{1,0:T(8,128)(2,1)}, u32[]{:S(2)}) copy-start(bf16[128,256]{1,0:T(8,128)(2,1)} %get-tuple-element.20) | copy-start | bytes 196612
  19.9 32.4 %copy-start = (f32[4096]{0:T(1024)S(1)}, f32[4096]{0:T(1024)}, u32[]{:S(2)}) copy-start(f32[4096]{0:T(1024)} %param.14) | copy-start | bytes 49156
  48.4 3.8 %collective-permute-start.2 = (bf16[4,2,128,256]{3,2,1,0:T(8,128)(2,1)S(1)}, bf16[4,2,128,256]{3,2,1,0:T(8,128)(2,1)S(1)}, u32[]{:S(2)}, u32[]{:S(2)}) collective-permute-start(bf16[4,2,128,256]{3,2,1,0:T(8,128)(2,1)S(1)} %all_to_all.15.own_ref), channel_id=1, source_target_pairs={{0,1},{1,0},{2,3},{3,2},{4,5},{5,4},{6,7},{7,6},{8,9},{9,8},{10,11... | collective-permute-start | bytes 1572872 | tf_op jit(solution)/shard_map/ppermute | solution.py:427
  54.3 14.7 %collective-permute-start.3 = (bf16[128,256]{1,0:T(8,128)(2,1)S(1)}, bf16[128,256]{1,0:T(8,128)(2,1)S(1)}, u32[]{:S(2)}, u32[]{:S(2)}) collective-permute-start(bf16[128,256]{1,0:T(8,128)(2,1)S(1)} %get-tuple-element.26), channel_id=1, source_target_pairs={{0,16},{16,0},{1,17},{17,1},{2,18},{18,2},{3,19},{19,3},{4,20},{20... | collective-permute-start | bytes 196616 | tf_op jit(solution)/shard_map/ppermute | solution.py:444
  56.2 38.9 %all-to-all-start.1 = ((bf16[8,128,128]{2,1,0:T(8,128)(2,1)}), bf16[8,128,128]{2,1,0:T(8,128)(2,1)S(1)}, u32[]{:S(2)}, u32[]{:S(2)}) async-start(bf16[8,128,128]{2,1,0:T(8,128)(2,1)} %get-tuple-element.24), calls=%async_computation.1 | async-start | bytes 524288 | tf_op jit(solution)/shard_map/all_to_all | solution.py:348

commit v3 on v2

--- a/solution.py
+++ b/solution.py
@@ -162,7 +162,8 @@
 
 def patch_kernel(
     rim_hbm, first_hbm, late_hbm, patch_hbm, cross_hbm, lift_hbm, kept_ref, leaving_ref,
-    rim_ref, first_ref, patch_ref, cross_ref, lift_ref, keys_ref, values_ref, local_ref, sems,
+    rim_ref, first_ref, late_ref, patch_ref, cross_ref, lift_ref,
+    keys_ref, values_ref, early_ref, local_ref, sems,
 ):
     ctx = lax.axis_index(CTX)
     half = first_ref.shape[1]
@@ -170,7 +171,7 @@
         (
             (rim_hbm, rim_ref),
             (first_hbm, first_ref),
-            (late_hbm, local_ref.at[pl.ds(half, half)]),
+            (late_hbm, late_ref),
             (patch_hbm, patch_ref),
             (cross_hbm, cross_ref),
             (lift_hbm, lift_ref),
@@ -178,25 +179,28 @@
         sems,
         0,
     )
-    for copy in copies:
+    local_ref[:, DH_L:] = jnp.ones((2 * half, DH_L), jnp.bfloat16)
+    for copy in copies[:2]:
         copy.wait()
     rim_bias = jnp.where(ctx > 0, 0.0, neg_large).astype(jnp.float32)
     keys_ref[:half] = rim_ref[:DH_L].T
     keys_ref[half:] = first_ref[DH_L : 2 * DH_L].T
     values_ref[:, :half] = rim_ref[DH_L:]
     values_ref[:, half:] = first_ref[2 * DH_L :]
-    window_attend(first_ref[:DH_L], keys_ref, values_ref, rim_bias, local_ref)
-    local_out = local_ref[...]
+    window_attend(first_ref[:DH_L], keys_ref, values_ref, rim_bias, early_ref)
+    for copy in copies[2:]:
+        copy.wait()
+    local_ref[:half, :DH_L] = early_ref[...]
+    local_ref[half:, :DH_L] = late_ref[...]
+    local_out = local_ref[:, :DH_L]
     quota = kept_ref.shape[0]
     slots = 2 * quota
     slot_of = patch_ref[...] - ctx * quota
     member = slot_of == lax.broadcasted_iota(jnp.int32, (slots, 2 * half), 0)
-    member_f = jnp.where(member, 1.0, 0.0)
-    counts = jnp.sum(member_f, axis=1, keepdims=True)
-    pooled = (
-        jnp.dot(member_f.astype(jnp.bfloat16), local_out, preferred_element_type=jnp.float32)
-        / jnp.maximum(counts, 1.0)
-    ).astype(jnp.bfloat16)
+    member_f = jnp.where(member, 1.0, 0.0).astype(jnp.bfloat16)
+    pooled = jnp.dot(member_f, local_ref[...], preferred_element_type=jnp.float32)
+    counts = pooled[:, DH_L : DH_L + 1]
+    pooled = (pooled[:, :DH_L] / jnp.maximum(counts, 1.0)).astype(jnp.bfloat16)
     keys = jnp.dot(
         local_out, cross_ref[:, :DH_L], preferred_element_type=jnp.float32
     ).astype(jnp.bfloat16)
@@ -207,8 +211,8 @@
         pooled, keys, (((1,), (1,)), ((), ())), preferred_element_type=jnp.float32
     )
     scores = jnp.where(member, scores, neg_large)
-    peak = jnp.max(scores, axis=1, keepdims=True)
-    weights = jnp.where(member, jnp.exp((scores - peak) * (1.0 / math.sqrt(DH_L))), 0.0)
+    peak = jnp.maximum(jnp.max(scores, axis=1, keepdims=True), 0.1 * neg_large)
+    weights = jnp.exp((scores - peak) * (1.0 / math.sqrt(DH_L)))
     normalizer = jnp.sum(weights, axis=1, keepdims=True)
     normalizer = jnp.where(normalizer > 0, normalizer, 1.0)
     attended = jnp.dot(
@@ -220,25 +224,42 @@
     leaving_ref[...] = patch_rows[quota:]
 
 
-def project_kernel(
-    own_ref, other_ref, gain_ref, w_ref, queries_ref, keep_ref, send_ref, scaled_ref
+def project_part(block_ref, block_core, gain_ref, w_ref, scaled_ref):
+    rows = block_ref.shape[2]
+    width = block_ref.shape[3]
+    squares = jnp.zeros((rows, 128), jnp.float32)
+    for yh in range(Y_HI):
+        for x in range(X):
+            block = block_ref[x, yh].astype(jnp.float32)
+            place = yh * X + x
+            first = pl.multiple_of((place * CORE + block_core) * width, width)
+            for lanes in range(0, width, 128):
+                piece = block[:, lanes : lanes + 128]
+                squares = squares + piece * piece
+            scaled_ref[:, place * width : (place + 1) * width] = (
+                block * gain_ref[:, pl.ds(first, width)]
+            ).astype(jnp.bfloat16)
+    weight = w_ref[:, block_core].reshape(scaled_ref.shape[1], w_ref.shape[3])
+    return jnp.dot(scaled_ref[...], weight, preferred_element_type=jnp.float32), squares
+
+
+def project_own_kernel(own_ref, gain_ref, w_ref, total_ref, squares_ref, scaled_ref):
+    core = lax.axis_index("core")
+    total, squares = project_part(own_ref, core, gain_ref, w_ref, scaled_ref)
+    total_ref[...] = total
+    squares_ref[...] = squares
+
+
+def project_other_kernel(
+    own_total_ref, own_squares_ref, other_ref, gain_ref, w_ref,
+    queries_ref, keep_ref, send_ref, scaled_ref,
 ):
     core = lax.axis_index("core")
     zl = lax.axis_index("zl")
-    rows = own_ref.shape[2]
-    width = own_ref.shape[3]
-    squares = jnp.zeros((rows, 128), jnp.float32)
-    for block_ref, block_core in ((own_ref, core), (other_ref, 1 - core)):
-        for x in range(X):
-            for yh in range(Y_HI):
-                block = block_ref[x, yh].astype(jnp.float32)
-                first = pl.multiple_of((yh * X * CORE + x * CORE + block_core) * width, width)
-                gain = gain_ref[:, pl.ds(first, width)]
-                for lanes in range(0, width, 128):
-                    piece = block[:, lanes : lanes + 128]
-                    squares = squares + piece * piece
-                scaled_ref[:, pl.ds(first, width)] = (block * gain).astype(jnp.bfloat16)
-    total = jnp.dot(scaled_ref[...], w_ref[...], preferred_element_type=jnp.float32)
+    rows = send_ref.shape[0]
+    total, squares = project_part(other_ref, 1 - core, gain_ref, w_ref, scaled_ref)
+    total = total + own_total_ref[...]
+    squares = squares + own_squares_ref[...]
     row_scale = lax.rsqrt(jnp.sum(squares, axis=1, keepdims=True) / DG + 1e-05)
     total = (total * row_scale).astype(jnp.bfloat16)
     for head in range(2):
@@ -249,14 +270,14 @@
 
         @pl.when(zl == head)
         def _():
-            keep_ref[...] = keys_vals
+            keep_ref[head * rows : (head + 1) * rows] = keys_vals
 
         @pl.when(zl != head)
         def _():
             send_ref[...] = keys_vals
 
 
-def attend_kernel(q_ref, kv_ref, out_ref, vt_ref, s_ref):
+def attend_kernel(q_ref, kv_ref, out_ref, vt_ref, s_ref, p_ref):
     y = lax.axis_index("yl")
     zh = lax.axis_index("zh")
     key_count = kv_ref.shape[0]
@@ -266,32 +287,31 @@
     vt_ref[...] = kv_ref[:, DH:].T
     chunk = 256
 
-    def attend(yy, masked):
+    def attend(yy, last):
+        reach = key_count if last is None else (last + 1) * chunk
         queries = q_ref[pl.ds(2 * yy, 2)].reshape(rows, DH)
-        peak = jnp.full((1, rows), neg_large, jnp.float32)
-        for first in range(0, key_count, chunk):
+        peak = jnp.full((8, rows), neg_large, jnp.float32)
+        for first in range(0, reach, chunk):
             scores = lax.dot_general(
                 kv_ref[first : first + chunk, :DH],
                 queries,
                 (((1,), (1,)), ((), ())),
                 preferred_element_type=jnp.float32,
             )
-            if masked:
-                key_at = first + lax.broadcasted_iota(jnp.int32, scores.shape, 0)
-                query_at = zh * rows + lax.broadcasted_iota(jnp.int32, scores.shape, 1)
+            if last is not None and first == last * chunk:
+                key_at = lax.broadcasted_iota(jnp.int32, scores.shape, 0)
+                query_at = lax.broadcasted_iota(jnp.int32, scores.shape, 1)
                 scores = jnp.where(key_at <= query_at, scores, neg_large)
             s_ref[first : first + chunk] = scores
-            peak = jnp.maximum(peak, jnp.max(scores, axis=0, keepdims=True))
-        normalizer = jnp.zeros((1, rows), jnp.float32)
-        summed = jnp.zeros((DH, rows), jnp.float32)
-        for first in range(0, key_count, chunk):
+            peak = jnp.maximum(peak, jnp.max(scores.reshape(chunk // 8, 8, rows), axis=0))
+        peak = jnp.max(peak, axis=0, keepdims=True)
+        normalizer = jnp.zeros((8, rows), jnp.float32)
+        for first in range(0, reach, chunk):
             weights = jnp.exp((s_ref[first : first + chunk] - peak) * scale)
-            normalizer = normalizer + jnp.sum(weights, axis=0, keepdims=True)
-            summed = summed + jnp.dot(
-                vt_ref[:, first : first + chunk],
-                weights.astype(jnp.bfloat16),
-                preferred_element_type=jnp.float32,
-            )
+            normalizer = normalizer + jnp.sum(weights.reshape(chunk // 8, 8, rows), axis=0)
+            p_ref[first : first + chunk] = weights.astype(jnp.bfloat16)
+        normalizer = jnp.sum(normalizer, axis=0, keepdims=True)
+        summed = jnp.dot(vt_ref[:, :reach], p_ref[:reach], preferred_element_type=jnp.float32)
         summed = (summed / normalizer).astype(jnp.bfloat16)
         level = peak * scale + jnp.log(normalizer)
         high = level.astype(jnp.bfloat16)
@@ -316,13 +336,15 @@
                 out_ref[2 * yy + part, :DH, :] = jnp.zeros((DH, half), jnp.bfloat16)
                 out_ref[2 * yy + part, DH:, :] = stats
 
-        @pl.when(yy == y)
-        def _():
-            attend(yy, True)
-
         @pl.when(yy > y)
         def _():
-            attend(yy, False)
+            attend(yy, None)
+
+    for last in range(Z_HALF):
+
+        @pl.when(zh == last)
+        def _():
+            attend(y, last)
 
 
 def merge_kernel(parts_ref, out_ref):
@@ -409,12 +431,17 @@
         scratch_shapes=[
             pltpu.VMEM(rim_shape, jnp.bfloat16),
             pltpu.VMEM((3 * DH_L, half), jnp.bfloat16),
+            pltpu.VMEM((half, DH_L), jnp.bfloat16),
             pltpu.VMEM((1, byte_count), jnp.int32),
             pltpu.VMEM(w_cross.shape[1:], jnp.bfloat16),
             pltpu.VMEM(w_patch.shape[1:], jnp.bfloat16),
         ]
         + window_scratch
-        + [pltpu.VMEM((byte_count, DH_L), jnp.bfloat16), pltpu.SemaphoreType.DMA((6,))],
+        + [
+            pltpu.VMEM((half, DH_L), jnp.bfloat16),
+            pltpu.VMEM((byte_count, 2 * DH_L), jnp.bfloat16),
+            pltpu.SemaphoreType.DMA((6,)),
+        ],
         compiler_params=pltpu.CompilerParams(vmem_limit_bytes=59 << 20),
         name="patches",
     )(rim, first_proj, late_out, byte_patch.reshape(1, -1), w_cross[0], w_patch[0])
@@ -425,27 +452,43 @@
     pair_rows = lax.all_gather(slab_rows, "yh", axis=0)
     own_rows = all_to_all_of(jnp.broadcast_to(pair_rows[None], (X,) + pair_rows.shape), "x")
     other_rows = lax.ppermute(own_rows, "core", [(0, 1), (1, 0)])
+    out_width = head_total * 3 * DH
+    split_weight = flat_weight.reshape(Y_HI * X, CORE, DG // (Y_HI * X * CORE), out_width)
+    gain_all = global_gain.reshape(1, DG)
+    cost = pl.CostEstimate(
+        flops=quota * DG * out_width, bytes_accessed=4 << 20, transcendentals=0
+    )
+    scaled_scratch = [pltpu.VMEM((quota, DG // CORE), jnp.bfloat16)]
+    own_total, own_squares = pl.pallas_call(
+        project_own_kernel,
+        out_shape=[
+            jax.ShapeDtypeStruct((quota, out_width), jnp.float32),
+            jax.ShapeDtypeStruct((quota, 128), jnp.float32),
+        ],
+        in_specs=[VMEM] * 3,
+        out_specs=[VMEM] * 2,
+        scratch_shapes=scaled_scratch,
+        compiler_params=pltpu.CompilerParams(vmem_limit_bytes=32 << 20),
+        cost_estimate=cost,
+        name="project_own",
+    )(own_rows, gain_all, split_weight)
     queries, kept_kv, sent_kv = pl.pallas_call(
-        project_kernel,
+        project_other_kernel,
         out_shape=[
             jax.ShapeDtypeStruct((Y_LO * Z_PAIR, quota, DH), jnp.bfloat16),
-            jax.ShapeDtypeStruct((quota, 2 * DH), jnp.bfloat16),
+            jax.ShapeDtypeStruct((2 * quota, 2 * DH), jnp.bfloat16),
             jax.ShapeDtypeStruct((quota, 2 * DH), jnp.bfloat16),
         ],
-        in_specs=[VMEM] * 4,
-        out_specs=[VMEM, VMEM, VMEM],
-        scratch_shapes=[pltpu.VMEM((quota, DG), jnp.bfloat16)],
+        in_specs=[VMEM] * 5,
+        out_specs=[VMEM] * 3,
+        scratch_shapes=scaled_scratch,
         compiler_params=pltpu.CompilerParams(vmem_limit_bytes=32 << 20),
-        cost_estimate=pl.CostEstimate(
-            flops=2 * quota * DG * head_total * 3 * DH, bytes_accessed=8 << 20, transcendentals=0
-        ),
-        name="project",
-    )(own_rows, other_rows, global_gain.reshape(1, DG), flat_weight)
+        cost_estimate=cost,
+        name="project_other",
+    )(own_total, own_squares, other_rows, gain_all, split_weight)
     swapped = lax.ppermute(sent_kv, "zl", [(0, 1), (1, 0)])
     queries = all_to_all_of(queries, ("yl", "zl"))
-    pair_kv = jnp.concatenate(
-        [jnp.where(zl == 0, kept_kv, swapped), jnp.where(zl == 0, swapped, kept_kv)], axis=0
-    )
+    pair_kv = lax.dynamic_update_slice_in_dim(kept_kv, swapped, (1 - zl) * quota, 0)
     keys_vals = lax.all_gather(pair_kv, "zh", axis=0, tiled=True)
     key_count = keys_vals.shape[0]
     partial_out = pl.pallas_call(
@@ -456,6 +499,7 @@
         scratch_shapes=[
             pltpu.VMEM((DH, key_count), jnp.bfloat16),
             pltpu.VMEM((key_count, 2 * quota), jnp.float32),
+            pltpu.VMEM((key_count, 2 * quota), jnp.bfloat16),
         ],
         compiler_params=pltpu.CompilerParams(vmem_limit_bytes=32 << 20),
         name="attend",

time: 112 us -> 112 us (level)
  waiting for transfers between devices: 1.89 us -> 4.14 us
  blocking collectives: 61.3 us -> 59.6 us
    ppermute x1, waiting for transfers between devices: 0.01 us -> 2.94 us  [local(): swapped = lax.ppermute(sent_kv, 'zl', [(0, 1), (1, 0)])]
    all_gather x1, blocking collectives: 26 us -> 23.5 us  [local(): keys_vals = lax.all_gather(pair_kv, 'zh', axis=0, tiled=True)]
    ppermute x1, starting transfers between devices: 1.91 us -> 3.92 us  [local(): swapped = lax.ppermute(sent_kv, 'zl', [(0, 1), (1, 0)])]
    all_to_all x1, starting transfers between devices: 12.8 us -> 11.3 us  [all_to_all_of(): return lax.all_to_all(block, axes, 0, 0, tiled=True)]
  transfers between devices with their start and end apart: 5 -> 5, of which waited for: 1 -> 2; matrix products, arithmetic and copies ran while one was open for 4% -> 4% of each run, Pallas kernels for 3% -> 4%
where the time goes in v3:
time: 112 us
  blocking collectives  59.6 us (53%)
  starting transfers between devices  25.7 us (23%)
  Pallas kernels  17.4 us (16%)
  local copies, waits for them, and re-layouts  4.6 us (4%)
  waiting for transfers between devices  4.14 us (4%)
    all_to_all x2, blocking collectives, all_to_all_of(): return lax.all_to_all(block, axes, 0, 0, tiled=True)  27.2 us
    all_gather x1, blocking collectives, local(): keys_vals = lax.all_gather(pair_kv, 'zh', axis=0, tiled=True)  23.5 us
    all_to_all x1, starting transfers between devices, all_to_all_of(): return lax.all_to_all(block, axes, 0, 0, tiled=True)  11.3 us
    all_gather x1, blocking collectives, local(): pair_rows = lax.all_gather(slab_rows, 'yh', axis=0)  8.85 us
    ppermute x2, starting transfers between devices, passed_along(): return lax.ppermute(block, axis, route)  8.55 us
    unnamed x7, local copies, waits for them, and re-layouts  4.56 us
    pallas_call x1, Pallas kernels, local(): pl.pallas_call(attend_kernel, out_shape=jax.ShapeDtypeStruct((Y_LO * Z_PA...  4.09 us
    pallas_call x1, Pallas kernels, local(): pl.pallas_call(patch_kernel, out_shape=[jax.ShapeDtypeStruct((quota, w_pa...  3.97 us
  transfers between devices with their start and end apart: 5, of which 2 were waited for; matrix products, arithmetic and copies ran while one was open for 4% of the time, Pallas kernels for 4%

profile of v3, /device:TPU:2, one launch (start us, length us, event | category | flops | bytes accessed | tf_op | source)
XLA Modules:
  0.0 111.5 jit_solution(13218579710120664648)
XLA Ops:
  0.0 2.8 %second_half.1 = (bf16[64,512]{1,0:T(8,128)(2,1)}, bf16[128,512]{1,0:T(8,128)(2,1)}) custom-call(bf16[1024,1024]{1,0:T(8,128)(2,1)} %states_ref.3, f32[1,1024]{1,0:T(1,128)} %bitcast.22, bf16[192,1024]{1,0:T(8,128)(2,1)} %bitcast.17), custom_call_target="tpu_custom_call" | custom-call | tf_op jit(solution)/shard_map/second_half/pallas_call | solution.py:393
  2.8 4.3 %collective-permute-start = (bf16[128,512]{1,0:T(8,128)(2,1)}, bf16[128,512]{1,0:T(8,128)(2,1)S(1)}, u32[]{:S(2)}, u32[]{:S(2)}) collective-permute-start(bf16[128,512]{1,0:T(8,128)(2,1)} %get-tuple-element.18.second_hbm), channel_id=1, source_target_pairs={{0,16},{16,32},{32,48},{48,64},{64,80},{80,96},{96,112},{112,128},... | collective-permute-start | bytes 393224 | tf_op jit(solution)/shard_map/ppermute | solution.py:28
  7.1 3.7 %first_half.1 = (bf16[192,512]{1,0:T(8,128)(2,1)}, bf16[512,64]{1,0:T(8,128)(2,1)}) custom-call(bf16[1024,1024]{1,0:T(8,128)(2,1)} %states_ref.3, f32[1,1024]{1,0:T(1,128)} %bitcast.23, bf16[192,1024]{1,0:T(8,128)(2,1)} %bitcast.18, bf16[64,512]{1,0:T(8,128)(2,1)} %get-tuple-element.19.query_hbm, bf16[128,512]{1,0:T(8,128)(2,1)} %get-tuple-element.18.second_hbm), custom_call_target="tpu_custom_call" | custom-call | flops 335544320 | bytes 8388608 | tf_op jit(solution)/shard_map/first_half/pallas_call | solution.py:406
  10.8 0.0 collective-permute-done.rim_hbm
  10.8 0.0 copy-start.1
  10.8 0.6 copy-done.1
  11.5 4.0 %patches.1 = (bf16[128,256]{1,0:T(8,128)(2,1)}, bf16[128,256]{1,0:T(8,128)(2,1)}) custom-call(bf16[128,512]{1,0:T(8,128)(2,1)} %copy-done.1, bf16[192,512]{1,0:T(8,128)(2,1)} %get-tuple-element.20.first_hbm, bf16[512,64]{1,0:T(8,128)(2,1)} %get-tuple-element.21.late_hbm, s32[1,1024]{1,0:T(1,128)} %bitcast.24, bf16[64,320]{1,0:T(8,128)(2,1)} %bitcast.20, ...), custom_call_target="tpu_custom_call" | custom-call | tf_op jit(solution)/shard_map/patches/pallas_call | solution.py:426
  15.5 4.3 %collective-permute-start.1 = (bf16[128,256]{1,0:T(8,128)(2,1)}, bf16[128,256]{1,0:T(8,128)(2,1)S(1)}, u32[]{:S(2)}, u32[]{:S(2)}) collective-permute-start(bf16[128,256]{1,0:T(8,128)(2,1)} %get-tuple-element.23), channel_id=1, source_target_pairs={{0,16},{16,32},{32,48},{48,64},{64,80},{80,96},{96,112},{112,128},... | collective-permute-start | bytes 196616 | tf_op jit(solution)/shard_map/ppermute | solution.py:28
  19.7 0.0 copy-start.2
  19.7 0.0 copy-start
  19.8 3.9 %copy.9 = bf16[512,8,2,384]{3,1,2,0:T(8,128)(2,1)S(1)} copy(bf16[512,8,2,384]{3,2,1,0:T(2,128)(2,1)} %bitcast.16) | data formatting | bytes 12582912
  23.7 0.0 collective-permute-done.1
  23.7 0.0 copy-done.2
  23.7 8.9 %all-gather = bf16[256,256]{1,0:T(8,128)(2,1)S(1)} all-gather(bf16[128,256]{1,0:T(8,128)(2,1)S(1)} %add.6), channel_id=2, replica_groups=mesh['yl'=4,'zh'=6,'zl'=2,'yh'=2,'x'=4,'core'=2] {'yh'}, dimensions={0}, use_global_device_ids=true | all-gather | bytes 196608 | tf_op jit(solution)/shard_map/all_gather | solution.py:452
  32.6 15.7 %all_to_all.15.own_ref = bf16[4,2,128,256]{3,2,1,0:T(8,128)(2,1)S(1)} all-to-all(bf16[4,2,128,256]{3,2,1,0:T(8,128)(2,1)S(1)} %broadcast_in_dim.2), channel_id=1, replica_groups=mesh['yl'=4,'zh'=6,'zl'=2,'yh'=2,'x'=4,'core'=2] {'x'}, dimensions={0} | all-to-all | bytes 1048576 | tf_op jit(solution)/shard_map/all_to_all | solution.py:370
  48.3 1.9 %collective-permute-start.2 = (bf16[4,2,128,256]{3,2,1,0:T(8,128)(2,1)S(1)}, bf16[4,2,128,256]{3,2,1,0:T(8,128)(2,1)S(1)}, u32[]{:S(2)}, u32[]{:S(2)}) collective-permute-start(bf16[4,2,128,256]{3,2,1,0:T(8,128)(2,1)S(1)} %all_to_all.15.own_ref), channel_id=1, source_target_pairs={{0,1},{1,0},{2,3},{3,2},{4,5},{5,4},{6,7},{7,6},{8,9},{9,8},{10,11... | collective-permute-start | bytes 1572872 | tf_op jit(solution)/shard_map/ppermute | solution.py:454
  50.2 0.0 copy-done
  50.2 0.7 project_own.1
  50.9 1.2 %collective-permute-done.2.other_ref = bf16[4,2,128,256]{3,2,1,0:T(8,128)(2,1)S(1)} collective-permute-done((bf16[4,2,128,256]{3,2,1,0:T(8,128)(2,1)S(1)}, bf16[4,2,128,256]{3,2,1,0:T(8,128)(2,1)S(1)}, u32[]{:S(2)}, u32[]{:S(2)}) %collective-permute-start.2) | collective-permute-done | bytes 524320 | tf_op jit(solution)/shard_map/ppermute | solution.py:454
  52.1 1.4 %project_other.1 = (bf16[8,128,128]{2,1,0:T(8,128)(2,1)}, bf16[256,256]{1,0:T(8,128)(2,1)S(1)}, bf16[128,256]{1,0:T(8,128)(2,1)S(1)}) custom-call(f32[128,768]{1,0:T(8,128)S(1)} %get-tuple-element.26.own_total_ref, f32[128,128]{1,0:T(8,128)S(1)} %get-tuple-element.27.own_squares_ref, bf16[4,2,128,256]{3,2,1,0:T(8,128)(2,1)S(1)} %collective-permute-done.2.other_ref, ...), custom_call_target="tpu_custom_call" | custom-call | flops 402653184 | bytes 4194304 | tf_op jit(solution)/shard_map/project_other/pallas_call | solution.py:475
  53.5 11.3 %all-to-all-start.1 = ((bf16[8,128,128]{2,1,0:T(8,128)(2,1)}), bf16[8,128,128]{2,1,0:T(8,128)(2,1)S(1)}, u32[]{:S(2)}, u32[]{:S(2)}) async-start(bf16[8,128,128]{2,1,0:T(8,128)(2,1)} %get-tuple-element.28), calls=%async_computation.1 | async-start | bytes 524288 | tf_op jit(solution)/shard_map/all_to_all | solution.py:370
  64.8 3.9 %collective-permute-start.3 = (bf16[128,256]{1,0:T(8,128)(2,1)S(1)}, bf16[128,256]{1,0:T(8,128)(2,1)S(1)}, u32[]{:S(2)}, u32[]{:S(2)}) collective-permute-start(bf16[128,256]{1,0:T(8,128)(2,1)S(1)} %get-tuple-element.30), channel_id=1, source_target_pairs={{0,16},{16,0},{1,17},{17,1},{2,18},{18,2},{3,19},{19,3},{4,20},{20... | collective-permute-start | bytes 196616 | tf_op jit(solution)/shard_map/ppermute | solution.py:489
  68.7 2.9 %collective-permute-done.3 = bf16[128,256]{1,0:T(8,128)(2,1)S(1)} collective-permute-done((bf16[128,256]{1,0:T(8,128)(2,1)S(1)}, bf16[128,256]{1,0:T(8,128)(2,1)S(1)}, u32[]{:S(2)}, u32[]{:S(2)}) %collective-permute-start.3) | collective-permute-done | bytes 65568 | tf_op jit(solution)/shard_map/ppermute | solution.py:489
  71.6 23.5 %all_gather.11.kv_ref = bf16[1536,256]{1,0:T(8,128)(2,1)S(1)} all-gather(bf16[256,256]{1,0:T(8,128)(2,1)S(1)} %constant_dynamic-update-slice_fusion), channel_id=1, replica_groups=mesh['yl'=4,'zh'=6,'zl'=2,'yh'=2,'x'=4,'core'=2] {'zh'}, dimensions={0}, use_global_device_ids=true | all-gather | bytes 917504 | tf_op jit(solution)/shard_map/all_gather | solution.py:492
  95.2 0.0 all-to-all-done.1.q_ref
  95.2 4.1 %attend.1 = bf16[8,144,128]{2,1,0:T(8,128)(2,1)S(1)} custom-call(bf16[8,128,128]{2,1,0:T(8,128)(2,1)S(1)} %all-to-all-done.1.q_ref, bf16[1536,256]{1,0:T(8,128)(2,1)S(1)} %all_gather.11.kv_ref), custom_call_target="tpu_custom_call" | custom-call | tf_op jit(solution)/shard_map/attend/pallas_call | solution.py:494
  99.3 11.5 %all_to_all.16.parts_ref = bf16[8,144,128]{2,1,0:T(8,128)(2,1)S(1)} all-to-all(bf16[8,144,128]{2,1,0:T(8,128)(2,1)S(1)} %attend.1), channel_id=1, replica_groups=mesh['yl'=4,'zh'=6,'zl'=2,'yh'=2,'x'=4,'core'=2] {'yl','zl'}, dimensions={0} | all-to-all | bytes 589824 | tf_op jit(solution)/shard_map/all_to_all | solution.py:370
  110.7 0.8 merge.1
  (3 shorter events, 0.1 us)
Async XLA Ops:
  2.8 8.0 %collective-permute-start = (bf16[128,512]{1,0:T(8,128)(2,1)}, bf16[128,512]{1,0:T(8,128)(2,1)S(1)}, u32[]{:S(2)}, u32[]{:S(2)}) collective-permute-start(bf16[128,512]{1,0:T(8,128)(2,1)} %get-tuple-element.18.second_hbm), channel_id=1, source_target_pairs={{0,16},{16,32},{32,48},{48,64},{64,80},{80,96},{96,112},{112,128},... | collective-permute-start | bytes 393224 | tf_op jit(solution)/shard_map/ppermute | solution.py:28
  10.8 0.7 copy-start.1
  15.5 8.2 %collective-permute-start.1 = (bf16[128,256]{1,0:T(8,128)(2,1)}, bf16[128,256]{1,0:T(8,128)(2,1)S(1)}, u32[]{:S(2)}, u32[]{:S(2)}) collective-permute-start(bf16[128,256]{1,0:T(8,128)(2,1)} %get-tuple-element.23), channel_id=1, source_target_pairs={{0,16},{16,32},{32,48},{48,64},{64,80},{80,96},{96,112},{112,128},... | collective-permute-start | bytes 196616 | tf_op jit(solution)/shard_map/ppermute | solution.py:28
  19.7 3.9 %copy-start.2 = (bf16[128,256]{1,0:T(8,128)(2,1)S(1)}, bf16[128,256]{1,0:T(8,128)(2,1)}, u32[]{:S(2)}) copy-start(bf16[128,256]{1,0:T(8,128)(2,1)} %get-tuple-element.22) | copy-start | bytes 196612
  19.7 30.5 %copy-start = (f32[4096]{0:T(1024)S(1)}, f32[4096]{0:T(1024)}, u32[]{:S(2)}) copy-start(f32[4096]{0:T(1024)} %param.14) | copy-start | bytes 49156
  48.3 3.8 %collective-permute-start.2 = (bf16[4,2,128,256]{3,2,1,0:T(8,128)(2,1)S(1)}, bf16[4,2,128,256]{3,2,1,0:T(8,128)(2,1)S(1)}, u32[]{:S(2)}, u32[]{:S(2)}) collective-permute-start(bf16[4,2,128,256]{3,2,1,0:T(8,128)(2,1)S(1)} %all_to_all.15.own_ref), channel_id=1, source_target_pairs={{0,1},{1,0},{2,3},{3,2},{4,5},{5,4},{6,7},{7,6},{8,9},{9,8},{10,11... | collective-permute-start | bytes 1572872 | tf_op jit(solution)/shard_map/ppermute | solution.py:454
  53.5 41.7 %all-to-all-start.1 = ((bf16[8,128,128]{2,1,0:T(8,128)(2,1)}), bf16[8,128,128]{2,1,0:T(8,128)(2,1)S(1)}, u32[]{:S(2)}, u32[]{:S(2)}) async-start(bf16[8,128,128]{2,1,0:T(8,128)(2,1)} %get-tuple-element.28), calls=%async_computation.1 | async-start | bytes 524288 | tf_op jit(solution)/shard_map/all_to_all | solution.py:370
  64.8 6.9 %collective-permute-start.3 = (bf16[128,256]{1,0:T(8,128)(2,1)S(1)}, bf16[128,256]{1,0:T(8,128)(2,1)S(1)}, u32[]{:S(2)}, u32[]{:S(2)}) collective-permute-start(bf16[128,256]{1,0:T(8,128)(2,1)S(1)} %get-tuple-element.30), channel_id=1, source_target_pairs={{0,16},{16,0},{1,17},{17,1},{2,18},{18,2},{3,19},{19,3},{4,20},{20... | collective-permute-start | bytes 196616 | tf_op jit(solution)/shard_map/ppermute | solution.py:489

commit v4 on v3

--- a/solution.py
+++ b/solution.py
@@ -256,7 +256,6 @@
 ):
     core = lax.axis_index("core")
     zl = lax.axis_index("zl")
-    rows = send_ref.shape[0]
     total, squares = project_part(other_ref, 1 - core, gain_ref, w_ref, scaled_ref)
     total = total + own_total_ref[...]
     squares = squares + own_squares_ref[...]
@@ -270,7 +269,7 @@
 
         @pl.when(zl == head)
         def _():
-            keep_ref[head * rows : (head + 1) * rows] = keys_vals
+            keep_ref[...] = keys_vals
 
         @pl.when(zl != head)
         def _():
@@ -289,6 +288,7 @@
 
     def attend(yy, last):
         reach = key_count if last is None else (last + 1) * chunk
+        slot = 0 if last is not None else yy % 2
         queries = q_ref[pl.ds(2 * yy, 2)].reshape(rows, DH)
         peak = jnp.full((8, rows), neg_large, jnp.float32)
         for first in range(0, reach, chunk):
@@ -302,16 +302,16 @@
                 key_at = lax.broadcasted_iota(jnp.int32, scores.shape, 0)
                 query_at = lax.broadcasted_iota(jnp.int32, scores.shape, 1)
                 scores = jnp.where(key_at <= query_at, scores, neg_large)
-            s_ref[first : first + chunk] = scores
+            s_ref[slot, first : first + chunk] = scores
             peak = jnp.maximum(peak, jnp.max(scores.reshape(chunk // 8, 8, rows), axis=0))
         peak = jnp.max(peak, axis=0, keepdims=True)
         normalizer = jnp.zeros((8, rows), jnp.float32)
         for first in range(0, reach, chunk):
-            weights = jnp.exp((s_ref[first : first + chunk] - peak) * scale)
+            weights = jnp.exp((s_ref[slot, first : first + chunk] - peak) * scale)
             normalizer = normalizer + jnp.sum(weights.reshape(chunk // 8, 8, rows), axis=0)
-            p_ref[first : first + chunk] = weights.astype(jnp.bfloat16)
+            p_ref[slot, first : first + chunk] = weights.astype(jnp.bfloat16)
         normalizer = jnp.sum(normalizer, axis=0, keepdims=True)
-        summed = jnp.dot(vt_ref[:, :reach], p_ref[:reach], preferred_element_type=jnp.float32)
+        summed = jnp.dot(vt_ref[:, :reach], p_ref[slot, :reach], preferred_element_type=jnp.float32)
         summed = (summed / normalizer).astype(jnp.bfloat16)
         level = peak * scale + jnp.log(normalizer)
         high = level.astype(jnp.bfloat16)
@@ -336,9 +336,12 @@
                 out_ref[2 * yy + part, :DH, :] = jnp.zeros((DH, half), jnp.bfloat16)
                 out_ref[2 * yy + part, DH:, :] = stats
 
-        @pl.when(yy > y)
+    for own in range(Y_LO - 1):
+
+        @pl.when(y == own)
         def _():
-            attend(yy, None)
+            for yy in range(own + 1, Y_LO):
+                attend(yy, None)
 
     for last in range(Z_HALF):
 
@@ -476,7 +479,7 @@
         project_other_kernel,
         out_shape=[
             jax.ShapeDtypeStruct((Y_LO * Z_PAIR, quota, DH), jnp.bfloat16),
-            jax.ShapeDtypeStruct((2 * quota, 2 * DH), jnp.bfloat16),
+            jax.ShapeDtypeStruct((quota, 2 * DH), jnp.bfloat16),
             jax.ShapeDtypeStruct((quota, 2 * DH), jnp.bfloat16),
         ],
         in_specs=[VMEM] * 5,
@@ -488,7 +491,9 @@
     )(own_total, own_squares, other_rows, gain_all, split_weight)
     swapped = lax.ppermute(sent_kv, "zl", [(0, 1), (1, 0)])
     queries = all_to_all_of(queries, ("yl", "zl"))
-    pair_kv = lax.dynamic_update_slice_in_dim(kept_kv, swapped, (1 - zl) * quota, 0)
+    pair_kv = jnp.concatenate(
+        [jnp.where(zl == 0, kept_kv, swapped), jnp.where(zl == 0, swapped, kept_kv)], axis=0
+    )
     keys_vals = lax.all_gather(pair_kv, "zh", axis=0, tiled=True)
     key_count = keys_vals.shape[0]
     partial_out = pl.pallas_call(
@@ -498,8 +503,8 @@
         out_specs=VMEM,
         scratch_shapes=[
             pltpu.VMEM((DH, key_count), jnp.bfloat16),
-            pltpu.VMEM((key_count, 2 * quota), jnp.float32),
-            pltpu.VMEM((key_count, 2 * quota), jnp.bfloat16),
+            pltpu.VMEM((2, key_count, 2 * quota), jnp.float32),
+            pltpu.VMEM((2, key_count, 2 * quota), jnp.bfloat16),
         ],
         compiler_params=pltpu.CompilerParams(vmem_limit_bytes=32 << 20),
         name="attend",

time: 112 us -> 109 us (0.973)
  waiting for transfers between devices: 4.14 us -> 1.2 us
  blocking collectives: 59.6 us -> 61.1 us
    ppermute x1, waiting for transfers between devices: 2.94 us -> 0.01 us  [local(): swapped = lax.ppermute(sent_kv, 'zl', [(0, 1), (1, 0)])]
    all_gather x1, blocking collectives: 23.5 us -> 26 us  [local(): keys_vals = lax.all_gather(pair_kv, 'zh', axis=0, tiled=True)]
    ppermute x1, starting transfers between devices: 3.92 us -> 1.91 us  [local(): swapped = lax.ppermute(sent_kv, 'zl', [(0, 1), (1, 0)])]
    all_to_all x1, starting transfers between devices: 11.3 us -> 12.8 us  [all_to_all_of(): return lax.all_to_all(block, axes, 0, 0, tiled=True)]
  transfers between devices with their start and end apart: 5 -> 5, of which waited for: 2 -> 1; matrix products, arithmetic and copies ran while one was open for 4% -> 4% of each run, Pallas kernels for 4% -> 4%
where the time goes in v4:
time: 109 us
  blocking collectives  61.1 us (56%)
  starting transfers between devices  25.2 us (23%)
  Pallas kernels  16.7 us (15%)
  local copies, waits for them, and re-layouts  4.59 us (4%)
  waiting for transfers between devices  1.2 us (1%)
    all_to_all x2, blocking collectives, all_to_all_of(): return lax.all_to_all(block, axes, 0, 0, tiled=True)  26.3 us
    all_gather x1, blocking collectives, local(): keys_vals = lax.all_gather(pair_kv, 'zh', axis=0, tiled=True)  26 us
    all_to_all x1, starting transfers between devices, all_to_all_of(): return lax.all_to_all(block, axes, 0, 0, tiled=True)  12.8 us
    all_gather x1, blocking collectives, local(): pair_rows = lax.all_gather(slab_rows, 'yh', axis=0)  8.85 us
    ppermute x2, starting transfers between devices, passed_along(): return lax.ppermute(block, axis, route)  8.56 us
    unnamed x7, local copies, waits for them, and re-layouts  4.55 us
    pallas_call x1, Pallas kernels, local(): pl.pallas_call(patch_kernel, out_shape=[jax.ShapeDtypeStruct((quota, w_pa...  3.96 us
    pallas_call x1, Pallas kernels, local(): pl.pallas_call(first_half_kernel, out_shape=[jax.ShapeDtypeStruct((3 * DH...  3.73 us
  transfers between devices with their start and end apart: 5, of which 1 were waited for; matrix products, arithmetic and copies ran while one was open for 4% of the time, Pallas kernels for 4%

profile of v4, /device:TPU:2, one launch (start us, length us, event | category | flops | bytes accessed | tf_op | source)
XLA Modules:
  0.0 109.0 jit_solution(15095024867973206714)
XLA Ops:
  0.0 2.8 %second_half.1 = (bf16[64,512]{1,0:T(8,128)(2,1)}, bf16[128,512]{1,0:T(8,128)(2,1)}) custom-call(bf16[1024,1024]{1,0:T(8,128)(2,1)} %states_ref.3, f32[1,1024]{1,0:T(1,128)} %bitcast.22, bf16[192,1024]{1,0:T(8,128)(2,1)} %bitcast.17), custom_call_target="tpu_custom_call" | custom-call | tf_op jit(solution)/shard_map/second_half/pallas_call | solution.py:396
  2.8 4.3 %collective-permute-start = (bf16[128,512]{1,0:T(8,128)(2,1)}, bf16[128,512]{1,0:T(8,128)(2,1)S(1)}, u32[]{:S(2)}, u32[]{:S(2)}) collective-permute-start(bf16[128,512]{1,0:T(8,128)(2,1)} %get-tuple-element.18.second_hbm), channel_id=1, source_target_pairs={{0,16},{16,32},{32,48},{48,64},{64,80},{80,96},{96,112},{112,128},... | collective-permute-start | bytes 393224 | tf_op jit(solution)/shard_map/ppermute | solution.py:28
  7.1 3.7 %first_half.1 = (bf16[192,512]{1,0:T(8,128)(2,1)}, bf16[512,64]{1,0:T(8,128)(2,1)}) custom-call(bf16[1024,1024]{1,0:T(8,128)(2,1)} %states_ref.3, f32[1,1024]{1,0:T(1,128)} %bitcast.23, bf16[192,1024]{1,0:T(8,128)(2,1)} %bitcast.18, bf16[64,512]{1,0:T(8,128)(2,1)} %get-tuple-element.19.query_hbm, bf16[128,512]{1,0:T(8,128)(2,1)} %get-tuple-element.18.second_hbm), custom_call_target="tpu_custom_call" | custom-call | flops 335544320 | bytes 8388608 | tf_op jit(solution)/shard_map/first_half/pallas_call | solution.py:409
  10.8 0.0 collective-permute-done.rim_hbm
  10.8 0.0 copy-start.1
  10.8 0.6 copy-done.1
  11.5 4.0 %patches.1 = (bf16[128,256]{1,0:T(8,128)(2,1)}, bf16[128,256]{1,0:T(8,128)(2,1)}) custom-call(bf16[128,512]{1,0:T(8,128)(2,1)} %copy-done.1, bf16[192,512]{1,0:T(8,128)(2,1)} %get-tuple-element.20.first_hbm, bf16[512,64]{1,0:T(8,128)(2,1)} %get-tuple-element.21.late_hbm, s32[1,1024]{1,0:T(1,128)} %bitcast.24, bf16[64,320]{1,0:T(8,128)(2,1)} %bitcast.20, ...), custom_call_target="tpu_custom_call" | custom-call | tf_op jit(solution)/shard_map/patches/pallas_call | solution.py:429
  15.4 4.3 %collective-permute-start.1 = (bf16[128,256]{1,0:T(8,128)(2,1)}, bf16[128,256]{1,0:T(8,128)(2,1)S(1)}, u32[]{:S(2)}, u32[]{:S(2)}) collective-permute-start(bf16[128,256]{1,0:T(8,128)(2,1)} %get-tuple-element.23), channel_id=1, source_target_pairs={{0,16},{16,32},{32,48},{48,64},{64,80},{80,96},{96,112},{112,128},... | collective-permute-start | bytes 196616 | tf_op jit(solution)/shard_map/ppermute | solution.py:28
  19.7 0.0 copy-start.2
  19.7 0.0 copy-start
  19.8 3.9 %copy.9 = bf16[512,8,2,384]{3,1,2,0:T(8,128)(2,1)S(1)} copy(bf16[512,8,2,384]{3,2,1,0:T(2,128)(2,1)} %bitcast.16) | data formatting | bytes 12582912
  23.7 0.0 collective-permute-done.1
  23.7 0.0 copy-done.2
  23.7 8.9 %all-gather = bf16[256,256]{1,0:T(8,128)(2,1)S(1)} all-gather(bf16[128,256]{1,0:T(8,128)(2,1)S(1)} %add.3), channel_id=2, replica_groups=mesh['yl'=4,'zh'=6,'zl'=2,'yh'=2,'x'=4,'core'=2] {'yh'}, dimensions={0}, use_global_device_ids=true | all-gather | bytes 196608 | tf_op jit(solution)/shard_map/all_gather | solution.py:455
  32.6 15.7 %all_to_all.15.own_ref = bf16[4,2,128,256]{3,2,1,0:T(8,128)(2,1)S(1)} all-to-all(bf16[4,2,128,256]{3,2,1,0:T(8,128)(2,1)S(1)} %broadcast_in_dim.2), channel_id=1, replica_groups=mesh['yl'=4,'zh'=6,'zl'=2,'yh'=2,'x'=4,'core'=2] {'x'}, dimensions={0} | all-to-all | bytes 1048576 | tf_op jit(solution)/shard_map/all_to_all | solution.py:373
  48.3 1.9 %collective-permute-start.2 = (bf16[4,2,128,256]{3,2,1,0:T(8,128)(2,1)S(1)}, bf16[4,2,128,256]{3,2,1,0:T(8,128)(2,1)S(1)}, u32[]{:S(2)}, u32[]{:S(2)}) collective-permute-start(bf16[4,2,128,256]{3,2,1,0:T(8,128)(2,1)S(1)} %all_to_all.15.own_ref), channel_id=1, source_target_pairs={{0,1},{1,0},{2,3},{3,2},{4,5},{5,4},{6,7},{7,6},{8,9},{9,8},{10,11... | collective-permute-start | bytes 1572872 | tf_op jit(solution)/shard_map/ppermute | solution.py:457
  50.2 0.0 copy-done
  50.2 0.7 project_own.1
  50.9 1.2 %collective-permute-done.2.other_ref = bf16[4,2,128,256]{3,2,1,0:T(8,128)(2,1)S(1)} collective-permute-done((bf16[4,2,128,256]{3,2,1,0:T(8,128)(2,1)S(1)}, bf16[4,2,128,256]{3,2,1,0:T(8,128)(2,1)S(1)}, u32[]{:S(2)}, u32[]{:S(2)}) %collective-permute-start.2) | collective-permute-done | bytes 524320 | tf_op jit(solution)/shard_map/ppermute | solution.py:457
  52.1 1.4 %project_other.1 = (bf16[8,128,128]{2,1,0:T(8,128)(2,1)}, bf16[128,256]{1,0:T(8,128)(2,1)S(1)}, bf16[128,256]{1,0:T(8,128)(2,1)S(1)}) custom-call(f32[128,768]{1,0:T(8,128)S(1)} %get-tuple-element.26.own_total_ref, f32[128,128]{1,0:T(8,128)S(1)} %get-tuple-element.27.own_squares_ref, bf16[4,2,128,256]{3,2,1,0:T(8,128)(2,1)S(1)} %collective-permute-done.2.other_ref, ...), custom_call_target="tpu_custom_call" | custom-call | flops 402653184 | bytes 4194304 | tf_op jit(solution)/shard_map/project_other/pallas_call | solution.py:478
  53.4 1.9 %collective-permute-start.3 = (bf16[128,256]{1,0:T(8,128)(2,1)S(1)}, bf16[128,256]{1,0:T(8,128)(2,1)S(1)}, u32[]{:S(2)}, u32[]{:S(2)}) collective-permute-start(bf16[128,256]{1,0:T(8,128)(2,1)S(1)} %get-tuple-element.30), channel_id=1, source_target_pairs={{0,16},{16,0},{1,17},{17,1},{2,18},{18,2},{3,19},{19,3},{4,20},{20... | collective-permute-start | bytes 196616 | tf_op jit(solution)/shard_map/ppermute | solution.py:492
  55.4 12.8 %all-to-all-start.1 = ((bf16[8,128,128]{2,1,0:T(8,128)(2,1)}), bf16[8,128,128]{2,1,0:T(8,128)(2,1)S(1)}, u32[]{:S(2)}, u32[]{:S(2)}) async-start(bf16[8,128,128]{2,1,0:T(8,128)(2,1)} %get-tuple-element.28), calls=%async_computation.1 | async-start | bytes 524288 | tf_op jit(solution)/shard_map/all_to_all | solution.py:373
  68.1 0.0 collective-permute-done.3
  68.2 26.0 %all_gather.11.kv_ref = bf16[1536,256]{1,0:T(8,128)(2,1)S(1)} all-gather(bf16[256,256]{1,0:T(8,128)(2,1)S(1)} %pad_maximum_fusion), channel_id=1, replica_groups=mesh['yl'=4,'zh'=6,'zl'=2,'yh'=2,'x'=4,'core'=2] {'zh'}, dimensions={0}, use_global_device_ids=true | all-gather | bytes 917504 | tf_op jit(solution)/shard_map/all_gather | solution.py:497
  94.2 0.0 all-to-all-done.1.q_ref
  94.2 3.4 %attend.1 = bf16[8,144,128]{2,1,0:T(8,128)(2,1)S(1)} custom-call(bf16[8,128,128]{2,1,0:T(8,128)(2,1)S(1)} %all-to-all-done.1.q_ref, bf16[1536,256]{1,0:T(8,128)(2,1)S(1)} %all_gather.11.kv_ref), custom_call_target="tpu_custom_call" | custom-call | tf_op jit(solution)/shard_map/attend/pallas_call | solution.py:499
  97.6 10.7 %all_to_all.16.parts_ref = bf16[8,144,128]{2,1,0:T(8,128)(2,1)S(1)} all-to-all(bf16[8,144,128]{2,1,0:T(8,128)(2,1)S(1)} %attend.1), channel_id=1, replica_groups=mesh['yl'=4,'zh'=6,'zl'=2,'yh'=2,'x'=4,'core'=2] {'yl','zl'}, dimensions={0} | all-to-all | bytes 589824 | tf_op jit(solution)/shard_map/all_to_all | solution.py:373
  108.2 0.8 merge.1
  (4 shorter events, 0.1 us)
Async XLA Ops:
  2.8 8.0 %collective-permute-start = (bf16[128,512]{1,0:T(8,128)(2,1)}, bf16[128,512]{1,0:T(8,128)(2,1)S(1)}, u32[]{:S(2)}, u32[]{:S(2)}) collective-permute-start(bf16[128,512]{1,0:T(8,128)(2,1)} %get-tuple-element.18.second_hbm), channel_id=1, source_target_pairs={{0,16},{16,32},{32,48},{48,64},{64,80},{80,96},{96,112},{112,128},... | collective-permute-start | bytes 393224 | tf_op jit(solution)/shard_map/ppermute | solution.py:28
  10.8 0.6 copy-start.1
  15.4 8.2 %collective-permute-start.1 = (bf16[128,256]{1,0:T(8,128)(2,1)}, bf16[128,256]{1,0:T(8,128)(2,1)S(1)}, u32[]{:S(2)}, u32[]{:S(2)}) collective-permute-start(bf16[128,256]{1,0:T(8,128)(2,1)} %get-tuple-element.23), channel_id=1, source_target_pairs={{0,16},{16,32},{32,48},{48,64},{64,80},{80,96},{96,112},{112,128},... | collective-permute-start | bytes 196616 | tf_op jit(solution)/shard_map/ppermute | solution.py:28
  19.7 3.9 %copy-start.2 = (bf16[128,256]{1,0:T(8,128)(2,1)S(1)}, bf16[128,256]{1,0:T(8,128)(2,1)}, u32[]{:S(2)}) copy-start(bf16[128,256]{1,0:T(8,128)(2,1)} %get-tuple-element.22) | copy-start | bytes 196612
  19.7 30.4 %copy-start = (f32[4096]{0:T(1024)S(1)}, f32[4096]{0:T(1024)}, u32[]{:S(2)}) copy-start(f32[4096]{0:T(1024)} %param.14) | copy-start | bytes 49156
  48.3 3.8 %collective-permute-start.2 = (bf16[4,2,128,256]{3,2,1,0:T(8,128)(2,1)S(1)}, bf16[4,2,128,256]{3,2,1,0:T(8,128)(2,1)S(1)}, u32[]{:S(2)}, u32[]{:S(2)}) collective-permute-start(bf16[4,2,128,256]{3,2,1,0:T(8,128)(2,1)S(1)} %all_to_all.15.own_ref), channel_id=1, source_target_pairs={{0,1},{1,0},{2,3},{3,2},{4,5},{5,4},{6,7},{7,6},{8,9},{9,8},{10,11... | collective-permute-start | bytes 1572872 | tf_op jit(solution)/shard_map/ppermute | solution.py:457
  53.4 14.7 %collective-permute-start.3 = (bf16[128,256]{1,0:T(8,128)(2,1)S(1)}, bf16[128,256]{1,0:T(8,128)(2,1)S(1)}, u32[]{:S(2)}, u32[]{:S(2)}) collective-permute-start(bf16[128,256]{1,0:T(8,128)(2,1)S(1)} %get-tuple-element.30), channel_id=1, source_target_pairs={{0,16},{16,0},{1,17},{17,1},{2,18},{18,2},{3,19},{19,3},{4,20},{20... | collective-permute-start | bytes 196616 | tf_op jit(solution)/shard_map/ppermute | solution.py:492
  55.4 38.8 %all-to-all-start.1 = ((bf16[8,128,128]{2,1,0:T(8,128)(2,1)}), bf16[8,128,128]{2,1,0:T(8,128)(2,1)S(1)}, u32[]{:S(2)}, u32[]{:S(2)}) async-start(bf16[8,128,128]{2,1,0:T(8,128)(2,1)} %get-tuple-element.28), calls=%async_computation.1 | async-start | bytes 524288 | tf_op jit(solution)/shard_map/all_to_all | solution.py:373

commit v5 on v4

--- a/solution.py
+++ b/solution.py
@@ -75,7 +75,7 @@
     rim_ref[...] = proj[DH_L:]
 
 
-def window_attend(queries_t, keys_ref, values_ref, early_bias, out_ref):
+def window_attend(queries_t, keys_ref, values_ref, early_bias, out_ref, features_first):
     scale = 1.0 / math.sqrt(DH_L)
     width = 128
     blocks = range(queries_t.shape[1] // width)
@@ -118,9 +118,12 @@
         for block in blocks
     ]
     for block in blocks:
-        out_ref[block * width : (block + 1) * width] = (
-            summed[block] / normalizers[block]
-        ).T.astype(jnp.bfloat16)
+        attended = summed[block] / normalizers[block]
+        lanes = slice(block * width, (block + 1) * width)
+        if features_first:
+            out_ref[:, lanes] = attended.astype(jnp.bfloat16)
+        else:
+            out_ref[lanes] = attended.T.astype(jnp.bfloat16)
 
 
 def started(pairs, sems, first):
@@ -133,17 +136,34 @@
     return copies
 
 
+PACK_LATE = 3 * DH_L
+PACK_SLOTS = PACK_LATE + DH_L
+PACK_CROSS = PACK_SLOTS + 16
+PACK_LIFT = PACK_CROSS + DH_L
+PACK_END = PACK_LIFT + DH_L
+
+
 def first_half_kernel(
-    states_ref, gain_hbm, w_hbm, query_hbm, second_hbm, first_ref, out_ref,
-    held_ref, normed_ref, gain_ref, w_ref, query_ref, second_ref, keys_ref, values_ref, sems,
+    states_ref, gain_hbm, w_hbm, query_hbm, second_hbm, patch_hbm, cross_hbm, lift_hbm, packed_ref,
+    held_ref, normed_ref, gain_ref, w_ref, query_ref, second_ref, patch_ref, cross_ref, lift_ref,
+    keys_ref, values_ref, sems,
 ):
-    half = first_ref.shape[1]
+    half = packed_ref.shape[1]
     parts = held_ref.shape[0]
     step = held_ref.shape[1]
     (gain_copy,) = started(((gain_hbm, gain_ref),), sems, parts)
     copies = rows_arriving(states_ref, held_ref, sems, 0)
     others = started(
-        ((second_hbm, second_ref), (w_hbm, w_ref), (query_hbm, query_ref)), sems, parts + 1
+        (
+            (second_hbm, second_ref),
+            (w_hbm, w_ref),
+            (query_hbm, query_ref),
+            (patch_hbm, patch_ref),
+            (cross_hbm, cross_ref),
+            (lift_hbm, lift_ref),
+        ),
+        sems,
+        parts + 1,
     )
     gain_copy.wait()
     for part, copy in enumerate(copies):
@@ -154,58 +174,53 @@
     keys_ref[half:] = second_ref[:DH_L].T
     values_ref[:, half:] = second_ref[DH_L:]
     proj = project_rows(w_ref, normed_ref)
-    first_ref[...] = proj
+    packed_ref[:PACK_LATE] = proj
     keys_ref[:half] = proj[DH_L : 2 * DH_L].T
     values_ref[:, :half] = proj[2 * DH_L :]
-    window_attend(query_ref[...], keys_ref, values_ref, None, out_ref)
+    slots = (patch_ref[...] - lax.axis_index(CTX) * (half // 4)).astype(jnp.float32)
+    row_at = lax.broadcasted_iota(jnp.int32, (16, half), 0)
+    packed_ref[PACK_SLOTS:PACK_CROSS] = jnp.where(
+        row_at == 0, slots[:, :half], jnp.where(row_at == 1, slots[:, half:], 0.0)
+    ).astype(jnp.bfloat16)
+    packed_ref[PACK_CROSS:PACK_LIFT, : cross_ref.shape[1]] = cross_ref[...]
+    packed_ref[PACK_LIFT:, : lift_ref.shape[1]] = lift_ref[...]
+    window_attend(
+        query_ref[...], keys_ref, values_ref, None, packed_ref.at[pl.ds(PACK_LATE, DH_L)], True
+    )
 
 
 def patch_kernel(
-    rim_hbm, first_hbm, late_hbm, patch_hbm, cross_hbm, lift_hbm, kept_ref, leaving_ref,
-    rim_ref, first_ref, late_ref, patch_ref, cross_ref, lift_ref,
-    keys_ref, values_ref, early_ref, local_ref, sems,
+    rim_ref, packed_ref, kept_ref, leaving_ref, keys_ref, values_ref, early_ref, local_ref
 ):
     ctx = lax.axis_index(CTX)
-    half = first_ref.shape[1]
-    copies = started(
-        (
-            (rim_hbm, rim_ref),
-            (first_hbm, first_ref),
-            (late_hbm, late_ref),
-            (patch_hbm, patch_ref),
-            (cross_hbm, cross_ref),
-            (lift_hbm, lift_ref),
-        ),
-        sems,
-        0,
-    )
+    half = packed_ref.shape[1]
     local_ref[:, DH_L:] = jnp.ones((2 * half, DH_L), jnp.bfloat16)
-    for copy in copies[:2]:
-        copy.wait()
     rim_bias = jnp.where(ctx > 0, 0.0, neg_large).astype(jnp.float32)
     keys_ref[:half] = rim_ref[:DH_L].T
-    keys_ref[half:] = first_ref[DH_L : 2 * DH_L].T
+    keys_ref[half:] = packed_ref[DH_L : 2 * DH_L].T
     values_ref[:, :half] = rim_ref[DH_L:]
-    values_ref[:, half:] = first_ref[2 * DH_L :]
-    window_attend(first_ref[:DH_L], keys_ref, values_ref, rim_bias, early_ref)
-    for copy in copies[2:]:
-        copy.wait()
+    values_ref[:, half:] = packed_ref[2 * DH_L : PACK_LATE]
+    window_attend(packed_ref[:DH_L], keys_ref, values_ref, rim_bias, early_ref, False)
     local_ref[:half, :DH_L] = early_ref[...]
-    local_ref[half:, :DH_L] = late_ref[...]
+    local_ref[half:, :DH_L] = packed_ref[PACK_LATE:PACK_SLOTS].T
     local_out = local_ref[:, :DH_L]
     quota = kept_ref.shape[0]
     slots = 2 * quota
-    slot_of = patch_ref[...] - ctx * quota
-    member = slot_of == lax.broadcasted_iota(jnp.int32, (slots, 2 * half), 0)
+    slot_rows = packed_ref[PACK_SLOTS:PACK_CROSS].astype(jnp.float32)
+    slot_of = jnp.concatenate([slot_rows[0:1], slot_rows[1:2]], axis=1)
+    member = slot_of == lax.broadcasted_iota(jnp.int32, (slots, 2 * half), 0).astype(jnp.float32)
+    lift_width = kept_ref.shape[1]
     member_f = jnp.where(member, 1.0, 0.0).astype(jnp.bfloat16)
     pooled = jnp.dot(member_f, local_ref[...], preferred_element_type=jnp.float32)
     counts = pooled[:, DH_L : DH_L + 1]
     pooled = (pooled[:, :DH_L] / jnp.maximum(counts, 1.0)).astype(jnp.bfloat16)
     keys = jnp.dot(
-        local_out, cross_ref[:, :DH_L], preferred_element_type=jnp.float32
+        local_out, packed_ref[PACK_CROSS:PACK_LIFT, :DH_L], preferred_element_type=jnp.float32
     ).astype(jnp.bfloat16)
     values = jnp.dot(
-        local_out, cross_ref[:, DH_L:], preferred_element_type=jnp.float32
+        local_out,
+        packed_ref[PACK_CROSS:PACK_LIFT, DH_L : DH_L + lift_width],
+        preferred_element_type=jnp.float32,
     ).astype(jnp.bfloat16)
     scores = lax.dot_general(
         pooled, keys, (((1,), (1,)), ((), ())), preferred_element_type=jnp.float32
@@ -218,7 +233,9 @@
     attended = jnp.dot(
         weights.astype(jnp.bfloat16), values, preferred_element_type=jnp.float32
     ) / normalizer
-    lifted = jnp.dot(pooled, lift_ref[...], preferred_element_type=jnp.float32)
+    lifted = jnp.dot(
+        pooled, packed_ref[PACK_LIFT:PACK_END, :lift_width], preferred_element_type=jnp.float32
+    )
     patch_rows = (lifted + attended).astype(jnp.bfloat16)
     kept_ref[...] = patch_rows[:quota]
     leaving_ref[...] = patch_rows[quota:]
@@ -406,18 +423,21 @@
         name="second_half",
     )(enc_states, gain_row, w_rows)
     rim = passed_along(rim_sent, CTX, 1)
-    first_proj, late_out = pl.pallas_call(
+    packed = pl.pallas_call(
         first_half_kernel,
-        out_shape=[
-            jax.ShapeDtypeStruct((3 * DH_L, half), jnp.bfloat16),
-            jax.ShapeDtypeStruct((half, DH_L), jnp.bfloat16),
-        ],
-        in_specs=[HBM] * 5,
-        out_specs=[VMEM] * 2,
+        out_shape=jax.ShapeDtypeStruct((PACK_END, half), jnp.bfloat16),
+        in_specs=[HBM] * 8,
+        out_specs=VMEM,
         scratch_shapes=held
-        + [pltpu.VMEM((DH_L, half), jnp.bfloat16), pltpu.VMEM(rim_shape, jnp.bfloat16)]
+        + [
+            pltpu.VMEM((DH_L, half), jnp.bfloat16),
+            pltpu.VMEM(rim_shape, jnp.bfloat16),
+            pltpu.VMEM((1, byte_count), jnp.int32),
+            pltpu.VMEM(w_cross.shape[1:], jnp.bfloat16),
+            pltpu.VMEM(w_patch.shape[1:], jnp.bfloat16),
+        ]
         + window_scratch
-        + [pltpu.SemaphoreType.DMA((8,))],
+        + [pltpu.SemaphoreType.DMA((11,))],
         compiler_params=pltpu.CompilerParams(vmem_limit_bytes=59 << 20),
         cost_estimate=pl.CostEstimate(
             flops=2 * half * byte_count * 3 * DH_L + 4 * half * byte_count * DH_L,
@@ -425,29 +445,23 @@
             transcendentals=half * byte_count,
         ),
         name="first_half",
-    )(enc_states, gain_row, w_rows, late_queries, rim_sent)
+    )(
+        enc_states, gain_row, w_rows, late_queries, rim_sent,
+        byte_patch.reshape(1, -1), w_cross[0], w_patch[0],
+    )
     kept_rows, leaving = pl.pallas_call(
         patch_kernel,
         out_shape=[jax.ShapeDtypeStruct((quota, w_patch.shape[2]), jnp.bfloat16)] * 2,
-        in_specs=[HBM] * 6,
+        in_specs=[VMEM] * 2,
         out_specs=[VMEM, VMEM],
-        scratch_shapes=[
-            pltpu.VMEM(rim_shape, jnp.bfloat16),
-            pltpu.VMEM((3 * DH_L, half), jnp.bfloat16),
-            pltpu.VMEM((half, DH_L), jnp.bfloat16),
-            pltpu.VMEM((1, byte_count), jnp.int32),
-            pltpu.VMEM(w_cross.shape[1:], jnp.bfloat16),
-            pltpu.VMEM(w_patch.shape[1:], jnp.bfloat16),
-        ]
-        + window_scratch
+        scratch_shapes=window_scratch
         + [
             pltpu.VMEM((half, DH_L), jnp.bfloat16),
             pltpu.VMEM((byte_count, 2 * DH_L), jnp.bfloat16),
-            pltpu.SemaphoreType.DMA((6,)),
         ],
-        compiler_params=pltpu.CompilerParams(vmem_limit_bytes=59 << 20),
+        compiler_params=pltpu.CompilerParams(vmem_limit_bytes=24 << 20),
         name="patches",
-    )(rim, first_proj, late_out, byte_patch.reshape(1, -1), w_cross[0], w_patch[0])
+    )(rim, packed)
     slab_rows = kept_rows + passed_along(leaving, CTX, 1)
     head_total = w_global.shape[1]
     flat_weight = w_global.reshape(DG, head_total * 3 * DH)

time: 109 us -> 108 us (level)
  Pallas kernels: 16.7 us -> 15 us
    pallas_call x1, Pallas kernels: 3.96 us -> 2.25 us  [local(): pl.pallas_call(patch_kernel, out_shape=[jax.ShapeDtypeStruct((quota, w_pa...]
    unnamed x7 -> x5, local copies, waits for them, and re-layouts: 4.55 us -> 4.88 us
where the time goes in v5:
time: 108 us
  blocking collectives  61.4 us (57%)
  starting transfers between devices  24.9 us (23%)
  Pallas kernels  15 us (14%)
  local copies, waits for them, and re-layouts  4.91 us (5%)
  waiting for transfers between devices  1.2 us (1%)
    all_to_all x2, blocking collectives, all_to_all_of(): return lax.all_to_all(block, axes, 0, 0, tiled=True)  26.4 us
    all_gather x1, blocking collectives, local(): keys_vals = lax.all_gather(pair_kv, 'zh', axis=0, tiled=True)  26.2 us
    all_to_all x1, starting transfers between devices, all_to_all_of(): return lax.all_to_all(block, axes, 0, 0, tiled=True)  12.5 us
    all_gather x1, blocking collectives, local(): pair_rows = lax.all_gather(slab_rows, 'yh', axis=0)  8.85 us
    ppermute x2, starting transfers between devices, passed_along(): return lax.ppermute(block, axis, route)  8.56 us
    unnamed x5, local copies, waits for them, and re-layouts  4.88 us
    pallas_call x1, Pallas kernels, local(): pl.pallas_call(first_half_kernel, out_shape=jax.ShapeDtypeStruct((PACK_EN...  3.77 us
    pallas_call x1, Pallas kernels, local(): pl.pallas_call(attend_kernel, out_shape=jax.ShapeDtypeStruct((Y_LO * Z_PA...  3.42 us
  transfers between devices with their start and end apart: 5, of which 1 were waited for; matrix products, arithmetic and copies ran while one was open for 4% of the time, Pallas kernels for 4%

profile of v5, /device:TPU:2, one launch (start us, length us, event | category | flops | bytes accessed | tf_op | source)
XLA Modules:
  0.0 107.7 jit_solution(1557884027361978099)
XLA Ops:
  0.0 2.8 %second_half.1 = (bf16[64,512]{1,0:T(8,128)(2,1)}, bf16[128,512]{1,0:T(8,128)(2,1)}) custom-call(bf16[1024,1024]{1,0:T(8,128)(2,1)} %states_ref.3, f32[1,1024]{1,0:T(1,128)} %bitcast.22, bf16[192,1024]{1,0:T(8,128)(2,1)} %bitcast.17), custom_call_target="tpu_custom_call" | custom-call | tf_op jit(solution)/shard_map/second_half/pallas_call | solution.py:413
  2.8 4.3 %collective-permute-start = (bf16[128,512]{1,0:T(8,128)(2,1)}, bf16[128,512]{1,0:T(8,128)(2,1)S(1)}, u32[]{:S(2)}, u32[]{:S(2)}) collective-permute-start(bf16[128,512]{1,0:T(8,128)(2,1)} %get-tuple-element.16.second_hbm), channel_id=1, source_target_pairs={{0,16},{16,32},{32,48},{48,64},{64,80},{80,96},{96,112},{112,128},... | collective-permute-start | bytes 393224 | tf_op jit(solution)/shard_map/ppermute | solution.py:28
  7.1 3.8 %first_half.1.packed_ref = bf16[400,512]{1,0:T(8,128)(2,1)} custom-call(bf16[1024,1024]{1,0:T(8,128)(2,1)} %states_ref.3, f32[1,1024]{1,0:T(1,128)} %bitcast.23, bf16[192,1024]{1,0:T(8,128)(2,1)} %bitcast.18, bf16[64,512]{1,0:T(8,128)(2,1)} %get-tuple-element.17.query_hbm, bf16[128,512]{1,0:T(8,128)(2,1)} %get-tuple-element.16.second_hbm, ...), custom_call_target="tpu_custom_call" | custom-call | flops 335544320 | bytes 8388608 | tf_op jit(solution)/shard_map/first_half/pallas_call | solution.py:426
  10.9 0.0 collective-permute-done.rim_ref
  10.9 0.0 copy-start
  10.9 1.0 copy-done
  11.9 2.2 %patches.1 = (bf16[128,256]{1,0:T(8,128)(2,1)S(1)}, bf16[128,256]{1,0:T(8,128)(2,1)S(1)}) custom-call(bf16[128,512]{1,0:T(8,128)(2,1)S(1)} %collective-permute-done.rim_ref, bf16[400,512]{1,0:T(8,128)(2,1)S(1)} %copy-done), custom_call_target="tpu_custom_call" | custom-call | tf_op jit(solution)/shard_map/patches/pallas_call | solution.py:452
  14.1 4.3 %collective-permute-start.1 = (bf16[128,256]{1,0:T(8,128)(2,1)S(1)}, bf16[128,256]{1,0:T(8,128)(2,1)S(1)}, u32[]{:S(2)}, u32[]{:S(2)}) collective-permute-start(bf16[128,256]{1,0:T(8,128)(2,1)S(1)} %get-tuple-element.19), channel_id=1, source_target_pairs={{0,16},{16,32},{32,48},{48,64},{64,80},{80,96},{96,112},{112,128},... | collective-permute-start | bytes 196616 | tf_op jit(solution)/shard_map/ppermute | solution.py:28
  18.4 0.0 copy-start.1
  18.4 3.9 %copy.9 = bf16[512,8,2,384]{3,1,2,0:T(8,128)(2,1)S(1)} copy(bf16[512,8,2,384]{3,2,1,0:T(2,128)(2,1)} %bitcast.16) | data formatting | bytes 12582912
  22.3 0.0 collective-permute-done.1
  22.3 8.9 %all-gather = bf16[256,256]{1,0:T(8,128)(2,1)S(1)} all-gather(bf16[128,256]{1,0:T(8,128)(2,1)S(1)} %add.3), channel_id=2, replica_groups=mesh['yl'=4,'zh'=6,'zl'=2,'yh'=2,'x'=4,'core'=2] {'yh'}, dimensions={0}, use_global_device_ids=true | all-gather | bytes 196608 | tf_op jit(solution)/shard_map/all_gather | solution.py:469
  31.2 15.7 %all_to_all.15.own_ref = bf16[4,2,128,256]{3,2,1,0:T(8,128)(2,1)S(1)} all-to-all(bf16[4,2,128,256]{3,2,1,0:T(8,128)(2,1)S(1)} %broadcast_in_dim.2), channel_id=1, replica_groups=mesh['yl'=4,'zh'=6,'zl'=2,'yh'=2,'x'=4,'core'=2] {'x'}, dimensions={0} | all-to-all | bytes 1048576 | tf_op jit(solution)/shard_map/all_to_all | solution.py:390
  47.0 1.9 %collective-permute-start.2 = (bf16[4,2,128,256]{3,2,1,0:T(8,128)(2,1)S(1)}, bf16[4,2,128,256]{3,2,1,0:T(8,128)(2,1)S(1)}, u32[]{:S(2)}, u32[]{:S(2)}) collective-permute-start(bf16[4,2,128,256]{3,2,1,0:T(8,128)(2,1)S(1)} %all_to_all.15.own_ref), channel_id=1, source_target_pairs={{0,1},{1,0},{2,3},{3,2},{4,5},{5,4},{6,7},{7,6},{8,9},{9,8},{10,11... | collective-permute-start | bytes 1572872 | tf_op jit(solution)/shard_map/ppermute | solution.py:471
  48.9 0.0 copy-done.1
  48.9 0.7 project_own.1
  49.6 1.2 %collective-permute-done.2.other_ref = bf16[4,2,128,256]{3,2,1,0:T(8,128)(2,1)S(1)} collective-permute-done((bf16[4,2,128,256]{3,2,1,0:T(8,128)(2,1)S(1)}, bf16[4,2,128,256]{3,2,1,0:T(8,128)(2,1)S(1)}, u32[]{:S(2)}, u32[]{:S(2)}) %collective-permute-start.2) | collective-permute-done | bytes 524320 | tf_op jit(solution)/shard_map/ppermute | solution.py:471
  50.8 1.4 %project_other.1 = (bf16[8,128,128]{2,1,0:T(8,128)(2,1)}, bf16[128,256]{1,0:T(8,128)(2,1)S(1)}, bf16[128,256]{1,0:T(8,128)(2,1)S(1)}) custom-call(f32[128,768]{1,0:T(8,128)S(1)} %get-tuple-element.22.own_total_ref, f32[128,128]{1,0:T(8,128)S(1)} %get-tuple-element.23.own_squares_ref, bf16[4,2,128,256]{3,2,1,0:T(8,128)(2,1)S(1)} %collective-permute-done.2.other_ref, ...), custom_call_target="tpu_custom_call" | custom-call | flops 402653184 | bytes 4194304 | tf_op jit(solution)/shard_map/project_other/pallas_call | solution.py:492
  52.1 1.9 %collective-permute-start.3 = (bf16[128,256]{1,0:T(8,128)(2,1)S(1)}, bf16[128,256]{1,0:T(8,128)(2,1)S(1)}, u32[]{:S(2)}, u32[]{:S(2)}) collective-permute-start(bf16[128,256]{1,0:T(8,128)(2,1)S(1)} %get-tuple-element.26), channel_id=1, source_target_pairs={{0,16},{16,0},{1,17},{17,1},{2,18},{18,2},{3,19},{19,3},{4,20},{20... | collective-permute-start | bytes 196616 | tf_op jit(solution)/shard_map/ppermute | solution.py:506
  54.1 12.5 %all-to-all-start.1 = ((bf16[8,128,128]{2,1,0:T(8,128)(2,1)}), bf16[8,128,128]{2,1,0:T(8,128)(2,1)S(1)}, u32[]{:S(2)}, u32[]{:S(2)}) async-start(bf16[8,128,128]{2,1,0:T(8,128)(2,1)} %get-tuple-element.24), calls=%async_computation.1 | async-start | bytes 524288 | tf_op jit(solution)/shard_map/all_to_all | solution.py:390
  66.6 0.0 collective-permute-done.3
  66.6 26.2 %all_gather.11.kv_ref = bf16[1536,256]{1,0:T(8,128)(2,1)S(1)} all-gather(bf16[256,256]{1,0:T(8,128)(2,1)S(1)} %pad_maximum_fusion), channel_id=1, replica_groups=mesh['yl'=4,'zh'=6,'zl'=2,'yh'=2,'x'=4,'core'=2] {'zh'}, dimensions={0}, use_global_device_ids=true | all-gather | bytes 917504 | tf_op jit(solution)/shard_map/all_gather | solution.py:511
  92.8 0.0 all-to-all-done.1.q_ref
  92.8 3.4 %attend.1 = bf16[8,144,128]{2,1,0:T(8,128)(2,1)S(1)} custom-call(bf16[8,128,128]{2,1,0:T(8,128)(2,1)S(1)} %all-to-all-done.1.q_ref, bf16[1536,256]{1,0:T(8,128)(2,1)S(1)} %all_gather.11.kv_ref), custom_call_target="tpu_custom_call" | custom-call | tf_op jit(solution)/shard_map/attend/pallas_call | solution.py:513
  96.2 10.7 %all_to_all.16.parts_ref = bf16[8,144,128]{2,1,0:T(8,128)(2,1)S(1)} all-to-all(bf16[8,144,128]{2,1,0:T(8,128)(2,1)S(1)} %attend.1), channel_id=1, replica_groups=mesh['yl'=4,'zh'=6,'zl'=2,'yh'=2,'x'=4,'core'=2] {'yl','zl'}, dimensions={0} | all-to-all | bytes 589824 | tf_op jit(solution)/shard_map/all_to_all | solution.py:390
  106.9 0.8 merge.1
  (4 shorter events, 0.1 us)
Async XLA Ops:
  2.8 8.1 %collective-permute-start = (bf16[128,512]{1,0:T(8,128)(2,1)}, bf16[128,512]{1,0:T(8,128)(2,1)S(1)}, u32[]{:S(2)}, u32[]{:S(2)}) collective-permute-start(bf16[128,512]{1,0:T(8,128)(2,1)} %get-tuple-element.16.second_hbm), channel_id=1, source_target_pairs={{0,16},{16,32},{32,48},{48,64},{64,80},{80,96},{96,112},{112,128},... | collective-permute-start | bytes 393224 | tf_op jit(solution)/shard_map/ppermute | solution.py:28
  10.9 1.0 copy-start
  14.1 8.2 %collective-permute-start.1 = (bf16[128,256]{1,0:T(8,128)(2,1)S(1)}, bf16[128,256]{1,0:T(8,128)(2,1)S(1)}, u32[]{:S(2)}, u32[]{:S(2)}) collective-permute-start(bf16[128,256]{1,0:T(8,128)(2,1)S(1)} %get-tuple-element.19), channel_id=1, source_target_pairs={{0,16},{16,32},{32,48},{48,64},{64,80},{80,96},{96,112},{112,128},... | collective-permute-start | bytes 196616 | tf_op jit(solution)/shard_map/ppermute | solution.py:28
  18.4 30.5 %copy-start.1 = (f32[4096]{0:T(1024)S(1)}, f32[4096]{0:T(1024)}, u32[]{:S(2)}) copy-start(f32[4096]{0:T(1024)} %param.14) | copy-start | bytes 49156
  47.0 3.8 %collective-permute-start.2 = (bf16[4,2,128,256]{3,2,1,0:T(8,128)(2,1)S(1)}, bf16[4,2,128,256]{3,2,1,0:T(8,128)(2,1)S(1)}, u32[]{:S(2)}, u32[]{:S(2)}) collective-permute-start(bf16[4,2,128,256]{3,2,1,0:T(8,128)(2,1)S(1)} %all_to_all.15.own_ref), channel_id=1, source_target_pairs={{0,1},{1,0},{2,3},{3,2},{4,5},{5,4},{6,7},{7,6},{8,9},{9,8},{10,11... | collective-permute-start | bytes 1572872 | tf_op jit(solution)/shard_map/ppermute | solution.py:471
  52.1 14.4 %collective-permute-start.3 = (bf16[128,256]{1,0:T(8,128)(2,1)S(1)}, bf16[128,256]{1,0:T(8,128)(2,1)S(1)}, u32[]{:S(2)}, u32[]{:S(2)}) collective-permute-start(bf16[128,256]{1,0:T(8,128)(2,1)S(1)} %get-tuple-element.26), channel_id=1, source_target_pairs={{0,16},{16,0},{1,17},{17,1},{2,18},{18,2},{3,19},{19,3},{4,20},{20... | collective-permute-start | bytes 196616 | tf_op jit(solution)/shard_map/ppermute | solution.py:506
  54.1 38.8 %all-to-all-start.1 = ((bf16[8,128,128]{2,1,0:T(8,128)(2,1)}), bf16[8,128,128]{2,1,0:T(8,128)(2,1)S(1)}, u32[]{:S(2)}, u32[]{:S(2)}) async-start(bf16[8,128,128]{2,1,0:T(8,128)(2,1)} %get-tuple-element.24), calls=%async_computation.1 | async-start | bytes 524288 | tf_op jit(solution)/shard_map/all_to_all | solution.py:390

commit v6 on v5

--- a/solution.py
+++ b/solution.py
@@ -40,7 +40,7 @@
 
 
 def norm_rows(states_ref, gain_ref, normed_ref):
-    step = 32
+    step = 16
     gain = gain_ref[...]
     for first in range(0, states_ref.shape[0], step):
         states = states_ref[first : first + step].astype(jnp.float32)
@@ -399,7 +399,7 @@
     model = enc_states.shape[1]
     HBM = pl.BlockSpec(memory_space=pltpu.HBM)
     held = [
-        pltpu.VMEM((4, half // 4, model), jnp.bfloat16),
+        pltpu.VMEM((2, half // 2, model), jnp.bfloat16),
         pltpu.VMEM((half, model), jnp.bfloat16),
         pltpu.VMEM((1, model), jnp.float32),
         pltpu.VMEM((3 * DH_L, model), jnp.bfloat16),
@@ -418,7 +418,7 @@
         ],
         in_specs=[HBM] * 3,
         out_specs=[VMEM] * 2,
-        scratch_shapes=held + [pltpu.SemaphoreType.DMA((6,))],
+        scratch_shapes=held + [pltpu.SemaphoreType.DMA((4,))],
         compiler_params=pltpu.CompilerParams(vmem_limit_bytes=59 << 20),
         name="second_half",
     )(enc_states, gain_row, w_rows)
@@ -437,7 +437,7 @@
             pltpu.VMEM(w_patch.shape[1:], jnp.bfloat16),
         ]
         + window_scratch
-        + [pltpu.SemaphoreType.DMA((11,))],
+        + [pltpu.SemaphoreType.DMA((9,))],
         compiler_params=pltpu.CompilerParams(vmem_limit_bytes=59 << 20),
         cost_estimate=pl.CostEstimate(
             flops=2 * half * byte_count * 3 * DH_L + 4 * half * byte_count * DH_L,

time: 108 us -> 108 us (level)
  no operation moved by 1% of the time
where the time goes in v6:
time: 108 us
  blocking collectives  61.6 us (57%)
  starting transfers between devices  24.9 us (23%)
  Pallas kernels  14.8 us (14%)
  local copies, waits for them, and re-layouts  4.91 us (5%)
  waiting for transfers between devices  1.2 us (1%)
    all_to_all x2, blocking collectives, all_to_all_of(): return lax.all_to_all(block, axes, 0, 0, tiled=True)  26.5 us
    all_gather x1, blocking collectives, local(): keys_vals = lax.all_gather(pair_kv, 'zh', axis=0, tiled=True)  26.2 us
    all_to_all x1, starting transfers between devices, all_to_all_of(): return lax.all_to_all(block, axes, 0, 0, tiled=True)  12.5 us
    all_gather x1, blocking collectives, local(): pair_rows = lax.all_gather(slab_rows, 'yh', axis=0)  8.85 us
    ppermute x2, starting transfers between devices, passed_along(): return lax.ppermute(block, axis, route)  8.55 us
    unnamed x5, local copies, waits for them, and re-layouts  4.88 us
    pallas_call x1, Pallas kernels, local(): pl.pallas_call(first_half_kernel, out_shape=jax.ShapeDtypeStruct((PACK_EN...  3.67 us
    pallas_call x1, Pallas kernels, local(): pl.pallas_call(attend_kernel, out_shape=jax.ShapeDtypeStruct((Y_LO * Z_PA...  3.41 us
  transfers between devices with their start and end apart: 5, of which 1 were waited for; matrix products, arithmetic and copies ran while one was open for 4% of the time, Pallas kernels for 4%

profile of v6, /device:TPU:2, one launch (start us, length us, event | category | flops | bytes accessed | tf_op | source)
XLA Modules:
  0.0 107.6 jit_solution(2846832731283100158)
XLA Ops:
  0.0 2.7 %second_half.1 = (bf16[64,512]{1,0:T(8,128)(2,1)}, bf16[128,512]{1,0:T(8,128)(2,1)}) custom-call(bf16[1024,1024]{1,0:T(8,128)(2,1)} %states_ref.3, f32[1,1024]{1,0:T(1,128)} %bitcast.22, bf16[192,1024]{1,0:T(8,128)(2,1)} %bitcast.17), custom_call_target="tpu_custom_call" | custom-call | tf_op jit(solution)/shard_map/second_half/pallas_call | solution.py:413
  2.7 4.3 %collective-permute-start = (bf16[128,512]{1,0:T(8,128)(2,1)}, bf16[128,512]{1,0:T(8,128)(2,1)S(1)}, u32[]{:S(2)}, u32[]{:S(2)}) collective-permute-start(bf16[128,512]{1,0:T(8,128)(2,1)} %get-tuple-element.16.second_hbm), channel_id=1, source_target_pairs={{0,16},{16,32},{32,48},{48,64},{64,80},{80,96},{96,112},{112,128},... | collective-permute-start | bytes 393224 | tf_op jit(solution)/shard_map/ppermute | solution.py:28
  7.0 3.7 %first_half.1.packed_ref = bf16[400,512]{1,0:T(8,128)(2,1)} custom-call(bf16[1024,1024]{1,0:T(8,128)(2,1)} %states_ref.3, f32[1,1024]{1,0:T(1,128)} %bitcast.23, bf16[192,1024]{1,0:T(8,128)(2,1)} %bitcast.18, bf16[64,512]{1,0:T(8,128)(2,1)} %get-tuple-element.17.query_hbm, bf16[128,512]{1,0:T(8,128)(2,1)} %get-tuple-element.16.second_hbm, ...), custom_call_target="tpu_custom_call" | custom-call | flops 335544320 | bytes 8388608 | tf_op jit(solution)/shard_map/first_half/pallas_call | solution.py:426
  10.7 0.0 collective-permute-done.rim_ref
  10.7 0.0 copy-start
  10.7 1.0 copy-done
  11.7 2.3 %patches.1 = (bf16[128,256]{1,0:T(8,128)(2,1)S(1)}, bf16[128,256]{1,0:T(8,128)(2,1)S(1)}) custom-call(bf16[128,512]{1,0:T(8,128)(2,1)S(1)} %collective-permute-done.rim_ref, bf16[400,512]{1,0:T(8,128)(2,1)S(1)} %copy-done), custom_call_target="tpu_custom_call" | custom-call | tf_op jit(solution)/shard_map/patches/pallas_call | solution.py:452
  13.9 4.3 %collective-permute-start.1 = (bf16[128,256]{1,0:T(8,128)(2,1)S(1)}, bf16[128,256]{1,0:T(8,128)(2,1)S(1)}, u32[]{:S(2)}, u32[]{:S(2)}) collective-permute-start(bf16[128,256]{1,0:T(8,128)(2,1)S(1)} %get-tuple-element.19), channel_id=1, source_target_pairs={{0,16},{16,32},{32,48},{48,64},{64,80},{80,96},{96,112},{112,128},... | collective-permute-start | bytes 196616 | tf_op jit(solution)/shard_map/ppermute | solution.py:28
  18.2 0.0 copy-start.1
  18.2 3.9 %copy.9 = bf16[512,8,2,384]{3,1,2,0:T(8,128)(2,1)S(1)} copy(bf16[512,8,2,384]{3,2,1,0:T(2,128)(2,1)} %bitcast.16) | data formatting | bytes 12582912
  22.1 0.0 collective-permute-done.1
  22.1 8.9 %all-gather = bf16[256,256]{1,0:T(8,128)(2,1)S(1)} all-gather(bf16[128,256]{1,0:T(8,128)(2,1)S(1)} %add.3), channel_id=2, replica_groups=mesh['yl'=4,'zh'=6,'zl'=2,'yh'=2,'x'=4,'core'=2] {'yh'}, dimensions={0}, use_global_device_ids=true | all-gather | bytes 196608 | tf_op jit(solution)/shard_map/all_gather | solution.py:469
  31.0 15.9 %all_to_all.15.own_ref = bf16[4,2,128,256]{3,2,1,0:T(8,128)(2,1)S(1)} all-to-all(bf16[4,2,128,256]{3,2,1,0:T(8,128)(2,1)S(1)} %broadcast_in_dim.2), channel_id=1, replica_groups=mesh['yl'=4,'zh'=6,'zl'=2,'yh'=2,'x'=4,'core'=2] {'x'}, dimensions={0} | all-to-all | bytes 1048576 | tf_op jit(solution)/shard_map/all_to_all | solution.py:390
  46.9 1.9 %collective-permute-start.2 = (bf16[4,2,128,256]{3,2,1,0:T(8,128)(2,1)S(1)}, bf16[4,2,128,256]{3,2,1,0:T(8,128)(2,1)S(1)}, u32[]{:S(2)}, u32[]{:S(2)}) collective-permute-start(bf16[4,2,128,256]{3,2,1,0:T(8,128)(2,1)S(1)} %all_to_all.15.own_ref), channel_id=1, source_target_pairs={{0,1},{1,0},{2,3},{3,2},{4,5},{5,4},{6,7},{7,6},{8,9},{9,8},{10,11... | collective-permute-start | bytes 1572872 | tf_op jit(solution)/shard_map/ppermute | solution.py:471
  48.8 0.0 copy-done.1
  48.8 0.7 project_own.1
  49.5 1.2 %collective-permute-done.2.other_ref = bf16[4,2,128,256]{3,2,1,0:T(8,128)(2,1)S(1)} collective-permute-done((bf16[4,2,128,256]{3,2,1,0:T(8,128)(2,1)S(1)}, bf16[4,2,128,256]{3,2,1,0:T(8,128)(2,1)S(1)}, u32[]{:S(2)}, u32[]{:S(2)}) %collective-permute-start.2) | collective-permute-done | bytes 524320 | tf_op jit(solution)/shard_map/ppermute | solution.py:471
  50.7 1.4 %project_other.1 = (bf16[8,128,128]{2,1,0:T(8,128)(2,1)}, bf16[128,256]{1,0:T(8,128)(2,1)S(1)}, bf16[128,256]{1,0:T(8,128)(2,1)S(1)}) custom-call(f32[128,768]{1,0:T(8,128)S(1)} %get-tuple-element.22.own_total_ref, f32[128,128]{1,0:T(8,128)S(1)} %get-tuple-element.23.own_squares_ref, bf16[4,2,128,256]{3,2,1,0:T(8,128)(2,1)S(1)} %collective-permute-done.2.other_ref, ...), custom_call_target="tpu_custom_call" | custom-call | flops 402653184 | bytes 4194304 | tf_op jit(solution)/shard_map/project_other/pallas_call | solution.py:492
  52.0 1.9 %collective-permute-start.3 = (bf16[128,256]{1,0:T(8,128)(2,1)S(1)}, bf16[128,256]{1,0:T(8,128)(2,1)S(1)}, u32[]{:S(2)}, u32[]{:S(2)}) collective-permute-start(bf16[128,256]{1,0:T(8,128)(2,1)S(1)} %get-tuple-element.26), channel_id=1, source_target_pairs={{0,16},{16,0},{1,17},{17,1},{2,18},{18,2},{3,19},{19,3},{4,20},{20... | collective-permute-start | bytes 196616 | tf_op jit(solution)/shard_map/ppermute | solution.py:506
  54.0 12.5 %all-to-all-start.1 = ((bf16[8,128,128]{2,1,0:T(8,128)(2,1)}), bf16[8,128,128]{2,1,0:T(8,128)(2,1)S(1)}, u32[]{:S(2)}, u32[]{:S(2)}) async-start(bf16[8,128,128]{2,1,0:T(8,128)(2,1)} %get-tuple-element.24), calls=%async_computation.1 | async-start | bytes 524288 | tf_op jit(solution)/shard_map/all_to_all | solution.py:390
  66.5 0.0 collective-permute-done.3
  66.5 26.2 %all_gather.11.kv_ref = bf16[1536,256]{1,0:T(8,128)(2,1)S(1)} all-gather(bf16[256,256]{1,0:T(8,128)(2,1)S(1)} %pad_maximum_fusion), channel_id=1, replica_groups=mesh['yl'=4,'zh'=6,'zl'=2,'yh'=2,'x'=4,'core'=2] {'zh'}, dimensions={0}, use_global_device_ids=true | all-gather | bytes 917504 | tf_op jit(solution)/shard_map/all_gather | solution.py:511
  92.7 0.0 all-to-all-done.1.q_ref
  92.7 3.4 %attend.1 = bf16[8,144,128]{2,1,0:T(8,128)(2,1)S(1)} custom-call(bf16[8,128,128]{2,1,0:T(8,128)(2,1)S(1)} %all-to-all-done.1.q_ref, bf16[1536,256]{1,0:T(8,128)(2,1)S(1)} %all_gather.11.kv_ref), custom_call_target="tpu_custom_call" | custom-call | tf_op jit(solution)/shard_map/attend/pallas_call | solution.py:513
  96.1 10.7 %all_to_all.16.parts_ref = bf16[8,144,128]{2,1,0:T(8,128)(2,1)S(1)} all-to-all(bf16[8,144,128]{2,1,0:T(8,128)(2,1)S(1)} %attend.1), channel_id=1, replica_groups=mesh['yl'=4,'zh'=6,'zl'=2,'yh'=2,'x'=4,'core'=2] {'yl','zl'}, dimensions={0} | all-to-all | bytes 589824 | tf_op jit(solution)/shard_map/all_to_all | solution.py:390
  106.8 0.8 merge.1
  (4 shorter events, 0.1 us)
Async XLA Ops:
  2.7 8.0 %collective-permute-start = (bf16[128,512]{1,0:T(8,128)(2,1)}, bf16[128,512]{1,0:T(8,128)(2,1)S(1)}, u32[]{:S(2)}, u32[]{:S(2)}) collective-permute-start(bf16[128,512]{1,0:T(8,128)(2,1)} %get-tuple-element.16.second_hbm), channel_id=1, source_target_pairs={{0,16},{16,32},{32,48},{48,64},{64,80},{80,96},{96,112},{112,128},... | collective-permute-start | bytes 393224 | tf_op jit(solution)/shard_map/ppermute | solution.py:28
  10.7 1.0 copy-start
  13.9 8.2 %collective-permute-start.1 = (bf16[128,256]{1,0:T(8,128)(2,1)S(1)}, bf16[128,256]{1,0:T(8,128)(2,1)S(1)}, u32[]{:S(2)}, u32[]{:S(2)}) collective-permute-start(bf16[128,256]{1,0:T(8,128)(2,1)S(1)} %get-tuple-element.19), channel_id=1, source_target_pairs={{0,16},{16,32},{32,48},{48,64},{64,80},{80,96},{96,112},{112,128},... | collective-permute-start | bytes 196616 | tf_op jit(solution)/shard_map/ppermute | solution.py:28
  18.2 30.6 %copy-start.1 = (f32[4096]{0:T(1024)S(1)}, f32[4096]{0:T(1024)}, u32[]{:S(2)}) copy-start(f32[4096]{0:T(1024)} %param.14) | copy-start | bytes 49156
  46.9 3.8 %collective-permute-start.2 = (bf16[4,2,128,256]{3,2,1,0:T(8,128)(2,1)S(1)}, bf16[4,2,128,256]{3,2,1,0:T(8,128)(2,1)S(1)}, u32[]{:S(2)}, u32[]{:S(2)}) collective-permute-start(bf16[4,2,128,256]{3,2,1,0:T(8,128)(2,1)S(1)} %all_to_all.15.own_ref), channel_id=1, source_target_pairs={{0,1},{1,0},{2,3},{3,2},{4,5},{5,4},{6,7},{7,6},{8,9},{9,8},{10,11... | collective-permute-start | bytes 1572872 | tf_op jit(solution)/shard_map/ppermute | solution.py:471
  52.0 14.4 %collective-permute-start.3 = (bf16[128,256]{1,0:T(8,128)(2,1)S(1)}, bf16[128,256]{1,0:T(8,128)(2,1)S(1)}, u32[]{:S(2)}, u32[]{:S(2)}) collective-permute-start(bf16[128,256]{1,0:T(8,128)(2,1)S(1)} %get-tuple-element.26), channel_id=1, source_target_pairs={{0,16},{16,0},{1,17},{17,1},{2,18},{18,2},{3,19},{19,3},{4,20},{20... | collective-permute-start | bytes 196616 | tf_op jit(solution)/shard_map/ppermute | solution.py:506
  54.0 38.8 %all-to-all-start.1 = ((bf16[8,128,128]{2,1,0:T(8,128)(2,1)}), bf16[8,128,128]{2,1,0:T(8,128)(2,1)S(1)}, u32[]{:S(2)}, u32[]{:S(2)}) async-start(bf16[8,128,128]{2,1,0:T(8,128)(2,1)} %get-tuple-element.24), calls=%async_computation.1 | async-start | bytes 524288 | tf_op jit(solution)/shard_map/all_to_all | solution.py:390
